TPU v7x, 32 devices: a whole 2x2x4 slice. The times are simulated.
32 devices in a mesh: fsdp: 32 (over z, y, x, core).
Axes of the slice: x: 2, y: 2, z: 4, core: 2. Of those that a mesh axis runs over, the one named last changes fastest.
Arguments:
- tokens: bfloat16 [8192, 768], P('fsdp'), may hold values from -6 to 6
- w_qkv: bfloat16 [768, 2304], P(None, 'fsdp'), may hold values from -0.21875 to 0.21875
- w_out: bfloat16 [768, 768], P(None, 'fsdp'), may hold values from -0.625 to 0.625
- w_up: bfloat16 [768, 2304], P(None, 'fsdp'), may hold values from -0.21875 to 0.21875
- w_down: bfloat16 [1152, 768], P(None, 'fsdp'), may hold values from -0.1875 to 0.1875
- gain_attn: bfloat16 [768], P('fsdp'), may hold values from 0.5 to 1.5
- gain_mlp: bfloat16 [768], P('fsdp'), may hold values from 0.5 to 1.5
- cotangent: bfloat16 [8192, 768], P('fsdp'), may hold values from -6 to 6
- block_counts: int32 [32], replicated, may hold values from 1 to 2, as said below
- seq_lengths: int32 [4], replicated, may hold values from 1024 to 2048, as said below
Outputs:
- block_out: bfloat16 [8192, 768], P('fsdp')
- tokens_grad: float32 [8192, 768], P('fsdp')
- w_qkv_grad: float32 [768, 2304], P(None, 'fsdp')
- w_out_grad: float32 [768, 768], P(None, 'fsdp')
- w_up_grad: float32 [768, 2304], P(None, 'fsdp')
- w_down_grad: float32 [1152, 768], P(None, 'fsdp')
- gain_attn_grad: float32 [768], P('fsdp')
- gain_mlp_grad: float32 [768], P('fsdp')
Inputs may be any that keep to these rules, and one draw needn't show every extreme that they name: `block_counts`: each device holds 1 to 2 blocks, 48 in all; some device holds 2. `seq_lengths`: the lengths add up to 6144; both 1024 and 2048 occur.
All inputs are finite; a program needn't handle non-finite values.
Results may differ from a plain program's by a relative error of at most 0.015.
Values may be sent and summed in bfloat16 or wider, within the bound.
No kernel may reach another device: no remote copies, remote signals or barrier semaphores. Data moves between devices by JAX's collectives and lax.ppermute only.
A program may use at most 128 MiB of HBM per device.

v0:
```python
import math

import jax
import jax.numpy as jnp
from jax import lax
from jax.experimental import pallas as pl
from jax.experimental.pallas import tpu as pltpu
from jax.sharding import PartitionSpec as P

D = 768
HEADS = 12
HD = 64
FF = 1152
BLK = 128
WIN = 64


EPSILON = 1e-05
MASKED = -1e30


def with_halo(shard, sides, width):
    for axis, dim in sides:
        peers, length = (lax.axis_size(axis), shard.shape[dim])
        up = [(i, (i + 1) % peers) for i in range(peers - 1)]
        down = [(j, i) for i, j in up]
        last = lax.slice_in_dim(shard, length - width, length, axis=dim)
        initial = lax.slice_in_dim(shard, 0, width, axis=dim)
        before = lax.ppermute(last, axis, up)
        after = lax.ppermute(initial, axis, down)
        shard = jnp.concatenate([before, shard, after], axis=dim)
    return shard


def norm_parts(values):
    center = values - jnp.mean(values, axis=-1, keepdims=True)
    factor = lax.rsqrt(jnp.mean(center * center, axis=-1, keepdims=True) + EPSILON)
    return (center * factor, factor)


def norm_back(grad_normed, normed, factor):
    return factor * (
        grad_normed
        - jnp.mean(grad_normed, axis=-1, keepdims=True)
        - normed * jnp.mean(grad_normed * normed, axis=-1, keepdims=True)
    )


def sequence_places(places, lengths):
    ends = jnp.cumsum(lengths)
    starts = ends - lengths
    segment = jnp.sum((places[:, None] >= ends[None, :]).astype(jnp.int32), axis=1)
    picked = segment[:, None] == jnp.arange(lengths.shape[0], dtype=jnp.int32)[None, :]
    start = jnp.sum(jnp.where(picked, starts[None, :], 0), axis=1)
    return (segment, places - start)


def rotary_tables(position):
    half = HD // 2
    freq = jnp.power(10000.0, -(jnp.arange(half, dtype=jnp.float32) * (2.0 / HD)))
    angle = position.astype(jnp.float32)[:, None] * freq[None, :]
    angle = jnp.concatenate([angle, angle], axis=1)[:, None, :]
    return (jnp.cos(angle), jnp.sin(angle))


def rotate_heads(values, cosine, sine):
    half = HD // 2
    turned = jnp.concatenate([-values[..., half:], values[..., :half]], axis=-1)
    return values * cosine + turned * sine


def rotate_back(grads, cosine, sine):
    half = HD // 2
    spun = grads * sine
    return grads * cosine + jnp.concatenate([spun[..., half:], -spun[..., :half]], axis=-1)


def rows_product(left, right):
    return lax.dot_general(
        left, right, (((0,), (0,)), ((), ())), preferred_element_type=jnp.float32
    )


def cols_product(left, right):
    return lax.dot_general(
        left, right, (((1,), (1,)), ((), ())), preferred_element_type=jnp.float32
    )


def exact_gelu(values):
    return jax.nn.gelu(values, approximate=False)


def masked_scores(query, key_heads, allowed, score_scale):
    raw_scores = (
        jnp.einsum("qhd,khd->hqk", query, key_heads, preferred_element_type=jnp.float32)
        * score_scale
    )
    return jnp.where(allowed[None], raw_scores, MASKED)


def column_term(grad_side, data_side):
    return rows_product(grad_side, data_side)


def permute(values, pairs):
    return lax.ppermute(values, "fsdp", pairs)


def links():
    sibling = [(i, i ^ 1) for i in range(32)]
    near = [(i, i ^ (2 if i & 1 else 4)) for i in range(32)]
    far = [(i, i ^ (4 if i & 1 else 2)) for i in range(32)]
    line = [[(i, (i + 8 * k) % 32) for i in range(32)] for k in range(4)]
    return (sibling, near, far, line)


def chip_place():
    me = lax.axis_index("fsdp")
    return (me // 8, (me // 4) % 2, (me // 2) % 2, me % 2)


def gather_rows(rows):
    return lax.all_gather(rows, "fsdp", axis=0, tiled=False)


def scatter_rows(terms):
    return lax.psum_scatter(terms, "fsdp", scatter_dimension=0, tiled=False).astype(jnp.float32)


def fold_pad(shard):
    count = shard.shape[-2]
    rest = shard[..., D:]
    half = (count + 1) // 2
    left, right = rest[..., :half, :], rest[..., half:, :]
    spare = [(0, 0)] * (shard.ndim - 2) + [(0, 2 * half - count), (0, 0)]
    rest = jnp.concatenate([left, jnp.pad(right, spare)], axis=-1)
    return jnp.concatenate([shard[..., :D], rest], axis=-2)


def unfold_pad(packed, count):
    half, lanes = (count + 1) // 2, FF - D
    rest = packed[..., count : count + half, :]
    rest = jnp.concatenate([rest[..., :lanes], rest[..., lanes:]], axis=-2)[..., :count, :]
    return jnp.concatenate([packed[..., :count, :], rest], axis=-1)


def body(
    tokens, w_qkv, w_out, w_up, w_down, gain_attn, gain_mlp, cotangent, block_counts, seq_lengths
):
    slot_total = tokens.shape[0]
    score_scale = 1.0 / math.sqrt(HD)
    device_index = lax.axis_index("fsdp")
    block_count = lax.dynamic_index_in_dim(block_counts, device_index, keepdims=False)
    device_ids = jnp.arange(block_counts.shape[0], dtype=jnp.int32)
    first_place = jnp.sum(jnp.where(device_ids < device_index, block_counts, 0)) * BLK
    live_rows = block_count * BLK
    stream_total = jnp.sum(block_counts) * BLK
    slot_index = jnp.arange(slot_total, dtype=jnp.int32)
    live_slots = slot_index < live_rows
    rim_offsets = jnp.arange(WIN, dtype=jnp.int32)
    query_place = first_place + slot_index
    before_place = first_place - WIN + rim_offsets
    after_place = first_place + live_rows + rim_offsets
    key_place = jnp.concatenate([before_place, query_place, after_place])
    key_live = jnp.concatenate([before_place >= 0, live_slots, after_place < stream_total])
    key_slot = jnp.concatenate([rim_offsets * 0 - 1, slot_index, rim_offsets * 0 - 1])
    query_seg, query_pos = sequence_places(query_place, seq_lengths)
    key_seg, unused = sequence_places(key_place, seq_lengths)
    in_window = jnp.abs(query_place[:, None] - key_place[None, :]) <= WIN
    allowed = live_slots[:, None] & key_live[None, :] & (
        query_seg[:, None] == key_seg[None, :]
    ) & in_window | jnp.logical_not(live_slots)[:, None] & (
        key_slot[None, :] == slot_index[:, None]
    )
    cosine, sine = rotary_tables(query_pos)
    peers = lax.axis_size("fsdp")
    columns = D // peers
    gains = jnp.zeros((8, D), jnp.bfloat16)
    gains = gains.at[0, :columns].set(gain_attn).at[1, :columns].set(gain_mlp)
    first_rows = gather_rows(jnp.concatenate([w_qkv.T, gains]))
    qkv_full = first_rows[:, : 3 * columns].reshape(3 * D, D)
    gain_a_full = first_rows[:, 3 * columns, :columns].reshape(D)
    gain_m_full = first_rows[:, 3 * columns + 1, :columns].reshape(D)
    up_columns = w_up.shape[1]
    later = jnp.concatenate([w_up.T, w_out.T, fold_pad(w_down.T)])
    later_rows = gather_rows(later)
    up_full = later_rows[:, :up_columns].reshape(2 * FF, D)
    out_full = later_rows[:, up_columns : up_columns + columns].reshape(D, D)
    down_full = unfold_pad(later_rows[:, up_columns + columns :], columns).reshape(D, FF)
    stream = tokens.astype(jnp.float32)
    normed_one, factor_one = norm_parts(stream)
    first_in = (normed_one * gain_a_full.astype(jnp.float32)).astype(jnp.bfloat16)
    joined = cols_product(first_in, qkv_full)
    query = rotate_heads(joined[:, :D].reshape(slot_total, HEADS, HD), cosine, sine).astype(
        jnp.bfloat16
    )
    keys_own = rotate_heads(
        joined[:, D : 2 * D].reshape(slot_total, HEADS, HD), cosine, sine
    ).astype(jnp.bfloat16)
    values_own = joined[:, 2 * D :].astype(jnp.bfloat16)
    pairs = jnp.concatenate([keys_own.reshape(slot_total, D), values_own], axis=1)
    edges = jnp.concatenate(
        [pairs[:WIN], lax.dynamic_slice_in_dim(pairs, live_rows - WIN, WIN, 0)], axis=0
    )
    framed = with_halo(edges, (("fsdp", 0),), WIN)
    all_pairs = jnp.concatenate([framed[:WIN], pairs, framed[3 * WIN :]], axis=0)
    key_heads = all_pairs[:, :D].reshape(-1, HEADS, HD)
    value_heads = all_pairs[:, D:].reshape(-1, HEADS, HD)
    scores = masked_scores(query, key_heads, allowed, score_scale)
    row_top = jnp.max(scores, axis=-1, keepdims=True)
    log_total = row_top + jnp.log(jnp.sum(jnp.exp(scores - row_top), axis=-1, keepdims=True))
    probs_low = jnp.exp(scores - log_total).astype(jnp.bfloat16)
    mixed = (
        jnp.einsum("hqk,khd->qhd", probs_low, value_heads, preferred_element_type=jnp.float32)
        .reshape(slot_total, D)
        .astype(jnp.bfloat16)
    )
    after_attn = stream + cols_product(mixed, out_full)
    normed_two, factor_two = norm_parts(after_attn)
    second_in = (normed_two * gain_m_full.astype(jnp.float32)).astype(jnp.bfloat16)
    projected = cols_product(second_in, up_full)
    gate_half = projected[:, FF:]
    activated, gelu_pull = jax.vjp(exact_gelu, projected[:, :FF])
    hidden = (activated * gate_half).astype(jnp.bfloat16)
    down_out = cols_product(hidden, down_full)
    block_out = jnp.where(live_slots[:, None], after_attn + down_out, 0.0).astype(jnp.bfloat16)
    out_grad = jnp.where(live_slots[:, None], cotangent, jnp.zeros_like(cotangent))
    d_hidden = jnp.dot(out_grad, down_full, preferred_element_type=jnp.float32)
    d_inputs = gelu_pull(d_hidden * gate_half)[0]
    d_projected = jnp.concatenate([d_inputs, d_hidden * activated], axis=1).astype(jnp.bfloat16)
    d_second = jnp.dot(d_projected, up_full, preferred_element_type=jnp.float32)
    grad_gain_m = jnp.sum(normed_two * d_second, axis=0)
    d_after = out_grad.astype(jnp.float32) + norm_back(
        d_second * gain_m_full.astype(jnp.float32), normed_two, factor_two
    )
    d_attn = d_after.astype(jnp.bfloat16)
    d_mixed = jnp.dot(d_attn, out_full, preferred_element_type=jnp.float32).astype(jnp.bfloat16).reshape(slot_total, HEADS, HD)
    scores = masked_scores(query, key_heads, allowed, score_scale)
    probs = jnp.exp(scores - log_total)
    d_probs = jnp.einsum("qhd,khd->hqk", d_mixed, value_heads, preferred_element_type=jnp.float32)
    d_scores = (probs * (d_probs - jnp.sum(probs * d_probs, axis=-1, keepdims=True))).astype(
        jnp.bfloat16
    )
    d_query = (
        jnp.einsum("hqk,khd->qhd", d_scores, key_heads, preferred_element_type=jnp.float32)
        * score_scale
    )
    d_keys = (
        jnp.einsum("hqk,qhd->khd", d_scores, query, preferred_element_type=jnp.float32)
        * score_scale
    )
    d_values = jnp.einsum(
        "hqk,qhd->khd", probs.astype(jnp.bfloat16), d_mixed, preferred_element_type=jnp.float32
    )
    d_pairs = jnp.concatenate([d_keys.reshape(-1, D), d_values.reshape(-1, D)], axis=1)
    grad_edges = jnp.concatenate([d_pairs[:WIN], d_pairs[WIN + slot_total :]], axis=0)
    returned = with_halo(grad_edges.astype(jnp.bfloat16), (("fsdp", 0),), WIN).astype(
        grad_edges.dtype
    )
    own_pairs = d_pairs[WIN : WIN + slot_total]
    own_pairs = own_pairs.at[:WIN].add(returned[:WIN])
    tail_rows = lax.dynamic_slice_in_dim(own_pairs, live_rows - WIN, WIN, 0) + returned[3 * WIN :]
    own_pairs = lax.dynamic_update_slice_in_dim(own_pairs, tail_rows, live_rows - WIN, 0)
    d_query_raw = rotate_back(d_query, cosine, sine).reshape(slot_total, D)
    d_keys_raw = rotate_back(own_pairs[:, :D].reshape(slot_total, HEADS, HD), cosine, sine).reshape(
        slot_total, D
    )
    d_joined = jnp.concatenate([d_query_raw, d_keys_raw, own_pairs[:, D:]], axis=1).astype(
        jnp.bfloat16
    )
    d_first = jnp.dot(d_joined, qkv_full, preferred_element_type=jnp.float32)
    grad_gain_a = jnp.sum(normed_one * d_first, axis=0)
    d_stream = d_after + norm_back(
        d_first * gain_a_full.astype(jnp.float32), normed_one, factor_one
    )
    tokens_grad = jnp.where(live_slots[:, None], d_stream, 0.0)
    down_terms = column_term(out_grad, hidden).astype(jnp.bfloat16).reshape(peers, columns, FF)
    up_terms = column_term(d_projected, second_in).astype(jnp.bfloat16)
    mlp_sum = scatter_rows(
        jnp.concatenate([up_terms.reshape(peers, up_columns, D), fold_pad(down_terms)], axis=1)
    )
    up_sum = mlp_sum[:up_columns].T
    down_sum = unfold_pad(mlp_sum[up_columns:], columns).T
    qkv_terms = column_term(d_joined, first_in).astype(jnp.bfloat16).reshape(peers, 3 * columns, D)
    out_terms = column_term(d_attn, mixed).astype(jnp.bfloat16).reshape(peers, columns, D)
    gain_terms = jnp.stack([grad_gain_a.reshape(peers, columns), grad_gain_m.reshape(peers, columns)], axis=1)
    gain_terms = jnp.pad(gain_terms.astype(jnp.bfloat16), ((0, 0), (0, 6), (0, D - columns)))
    attn_sum = scatter_rows(jnp.concatenate([qkv_terms, out_terms, gain_terms], axis=1))
    qkv_sum = attn_sum[: 3 * columns].T
    out_sum = attn_sum[3 * columns : 4 * columns].T
    gain_a_sum = attn_sum[4 * columns, :columns]
    gain_m_sum = attn_sum[4 * columns + 1, :columns]
    return (block_out, tokens_grad, qkv_sum, out_sum, up_sum, down_sum, gain_a_sum, gain_m_sum)


CHIPS = 16
HALF = 384
ROWS1 = 160
ROWS2 = 272
SLOTS = 256
SPAN = SLOTS + 2 * WIN
PAIR = 2 * HD
PAIRS = HEADS // 2
LIMIT = 48 * 1024 * 1024
AT_LIVE, AT_CORE, AT_CHIP, AT_PUT = 0, 1, 2, 34
VMEM = pltpu.MemorySpace.VMEM
SMEM = pltpu.MemorySpace.SMEM


def nt_dot(left, right):
    return lax.dot_general(left, right, (((1,), (1,)), ((), ())), preferred_element_type=jnp.float32)


def nn_dot(left, right):
    return jnp.dot(left, right, preferred_element_type=jnp.float32)


def tn_dot(left, right):
    return lax.dot_general(left, right, (((0,), (0,)), ((), ())), preferred_element_type=jnp.float32)


def call(kernel, outs, scratch, args, micros, blocks=0):
    whole = len(args) - blocks - 1
    spaces = [pl.BlockSpec(memory_space=SMEM)] + [pl.BlockSpec(memory_space=VMEM)] * whole
    spaces += [pl.BlockSpec(memory_space=pl.ANY)] * blocks
    semaphores = [pltpu.SemaphoreType.DMA((2 * CHIPS, 4))] if blocks else []
    return pl.pallas_call(
        kernel,
        out_shape=[jax.ShapeDtypeStruct(shape, kind) for shape, kind in outs],
        in_specs=spaces,
        out_specs=[pl.BlockSpec(memory_space=VMEM)] * len(outs),
        scratch_shapes=[pltpu.VMEM(shape, kind) for shape, kind in scratch] + semaphores,
        compiler_params=pltpu.CompilerParams(vmem_limit_bytes=LIMIT),
        cost_estimate=pl.CostEstimate(flops=0, bytes_accessed=3_690_000 * micros, transcendentals=0),
    )(*args)


def block_copies(place, refs, weight, done, kind, start, count):
    copies = []
    for slot in range(2 * CHIPS):
        chip = place[AT_CHIP + slot]
        core = place[AT_CORE] if slot < CHIPS else 1 - place[AT_CORE]
        rows = pl.ds(pl.multiple_of(chip * count, 16), count)
        lanes = pl.ds(pl.multiple_of(core * HALF, 128), HALF)
        source = refs[slot // 4].at[slot % 4, start : start + count, :]
        copies.append(pltpu.make_async_copy(source, weight.at[rows, lanes], done.at[slot, kind]))
    return copies


def rest_copies(place, refs, weight, done, core):
    copies = []
    for slot in range(2 * CHIPS):
        stream = core if slot < CHIPS else 1 - core
        count = 32 if stream == 0 else 16
        first = pl.multiple_of(place[AT_CHIP + slot] * 48 + (0 if stream == 0 else 32), 16)
        source = refs[slot // 4].at[slot % 4, 240 : 240 + count, :]
        copies.append(
            pltpu.make_async_copy(source, weight.at[pl.ds(first, count), 2 * HALF :], done.at[slot, 3])
        )
    return copies


def go(copies):
    for copy in copies:
        copy.start()


def land(copies):
    for copy in copies:
        copy.wait()


def put_rows(place, send, keep, stream, start, value, chips):
    count = value.shape[0] // len(chips)
    value = value.astype(jnp.bfloat16)

    def store(ref):
        for i, chip in enumerate(chips):
            slot = place[AT_PUT + 16 * stream + chip]
            ref[slot, start : start + count, :] = value[i * count : (i + 1) * count]

    pl.when(place[AT_CORE] == stream)(lambda: store(keep))
    pl.when(place[AT_CORE] != stream)(lambda: store(send))


def put_both(place, send, keep, start, value, chips):
    for stream in (0, 1):
        put_rows(place, send, keep, stream, start, value[:, HALF * stream : HALF * (stream + 1)], chips)


def gain_rows(vector, chip):
    start = min(48 * chip // 128 * 128, D - HALF)
    return jnp.broadcast_to(vector[:, start : start + HALF], (16, HALF))


def project_kernel(place, tokens, gain, cos, sin_a, sin_b, *rest):
    refs, (query, pairs, first, weight, done) = rest[:8], rest[8:]
    copies = block_copies(place, refs, weight, done, 0, 0, 144)
    go(copies)
    normed, _ = norm_parts(tokens[...].astype(jnp.float32))
    a1 = (normed * gain[...]).astype(jnp.bfloat16)
    first[...] = a1
    c, sa, sb = cos[...], sin_a[...], sin_b[...]
    land(copies)
    for part in range(3):
        for j in range(2):
            base = part * D + HALF * j
            joined = nt_dot(a1, weight[base : base + HALF, :])
            for p in range(3):
                lanes = slice(HALF * j + PAIR * p, HALF * j + PAIR * (p + 1))
                v = joined[:, PAIR * p : PAIR * (p + 1)]
                if part < 2:
                    v = v * c + pltpu.roll(v, 96, 1) * sa + pltpu.roll(v, 32, 1) * sb
                if part == 0:
                    query[:, lanes] = v.astype(jnp.bfloat16)
                else:
                    where = slice((part - 1) * D + lanes.start, (part - 1) * D + lanes.stop)
                    pairs[:, where] = v.astype(jnp.bfloat16)


def frame_pairs(place, pairs, before, after, framed):
    framed[0:WIN, :] = before[...]
    framed[WIN : WIN + SLOTS, :] = pairs[...]
    framed[WIN + SLOTS : SPAN, :] = jnp.zeros((WIN, 2 * D), jnp.bfloat16)
    framed[pl.ds(pl.multiple_of(WIN + place[AT_LIVE], 64), WIN), :] = after[...]


def stack_heads(values, low, high):
    return jnp.concatenate([values * low, values * high], axis=0)


def head_masks():
    lane = lax.broadcasted_iota(jnp.int32, (1, PAIR), 1)
    low = jnp.where(lane < HD, 1.0, 0.0).astype(jnp.bfloat16)
    return (lane < HD, low, 1.0 - low)


def probabilities(query, keys, bias):
    scores = nt_dot(query, keys) * (1.0 / math.sqrt(HD)) + bias
    expos = jnp.exp(scores - jnp.max(scores, axis=-1, keepdims=True))
    return expos * (1.0 / jnp.sum(expos, axis=-1, keepdims=True))


def attend_kernel(place, query, pairs, before, after, bias, mixed, framed):
    frame_pairs(place, pairs, before, after, framed)
    is_low, low, high = head_masks()
    for block in range(2):
        rows, keys = slice(128 * block, 128 * block + 128), slice(128 * block, 128 * block + 256)
        both = jnp.concatenate([bias[rows, :], bias[rows, :]], axis=0)
        for p in range(PAIRS):
            lanes, vlanes = slice(PAIR * p, PAIR * (p + 1)), slice(D + PAIR * p, D + PAIR * (p + 1))
            probs = probabilities(stack_heads(query[rows, lanes], low, high), framed[keys, lanes], both)
            out = nn_dot(probs.astype(jnp.bfloat16), framed[keys, vlanes])
            mixed[rows, lanes] = jnp.where(is_low, out[:128], out[128:]).astype(jnp.bfloat16)


def middle_kernel(place, tokens, mixed, gain, cotangent, *rest):
    refs = rest[:8]
    block_out, d_after_out, d_mixed, send, keep, w_up, w_out, w_down, d_proj, hidden, done = rest[8:]
    out_copies = block_copies(place, refs, w_out, done, 0, 144, 48)
    up_copies = block_copies(place, refs, w_up, done, 1, 0, 144)
    down_copies = block_copies(place, refs, w_down, done, 2, 192, 48)
    go(out_copies)
    go(up_copies)
    go(down_copies)
    for core in (0, 1):
        pl.when(place[AT_CORE] == core)(lambda: go(rest_copies(place, refs, w_down, done, core)))
    land(out_copies)
    after_attn = tokens[...].astype(jnp.float32) + nt_dot(mixed[...], w_out[...])
    normed, factor = norm_parts(after_attn)
    gains = gain[...]
    a2 = (normed * gains).astype(jnp.bfloat16)
    live = lax.broadcasted_iota(jnp.int32, (SLOTS, 1), 0) < place[AT_LIVE]
    grad = jnp.where(live, cotangent[...].astype(jnp.float32), 0.0)
    out_grad = grad.astype(jnp.bfloat16)
    down = jnp.zeros((SLOTS, D), jnp.float32)
    land(up_copies)
    land(down_copies)
    for core in (0, 1):
        pl.when(place[AT_CORE] == core)(lambda: land(rest_copies(place, refs, w_down, done, core)))
    for j in range(3):
        lanes = slice(HALF * j, HALF * (j + 1))
        inputs = nt_dot(a2, w_up[lanes, :])
        gate = nt_dot(a2, w_up[FF + HALF * j : FF + HALF * (j + 1), :])
        cdf = 0.5 * (1.0 + lax.erf(inputs * (1.0 / math.sqrt(2.0))))
        slope = cdf + inputs * (jnp.exp(-0.5 * inputs * inputs) * (1.0 / math.sqrt(2.0 * math.pi)))
        active = inputs * cdf
        low_hidden = (active * gate).astype(jnp.bfloat16)
        hidden[:, lanes] = low_hidden
        down = down + nt_dot(low_hidden, w_down[:, lanes])
        d_hidden = nn_dot(out_grad, w_down[:, lanes])
        d_proj[:, lanes] = (d_hidden * gate * slope).astype(jnp.bfloat16)
        d_proj[:, FF + HALF * j : FF + HALF * (j + 1)] = (d_hidden * active).astype(jnp.bfloat16)
    block_out[...] = jnp.where(live, after_attn + down, 0.0).astype(jnp.bfloat16)
    everyone = list(range(CHIPS))
    d_second = nn_dot(d_proj[...], w_up[...])
    gain_grad = jnp.sum(normed * d_second, axis=0, keepdims=True)
    d_after = grad + norm_back(d_second * gains, normed, factor)
    d_after_out[...] = d_after
    d_attn = d_after.astype(jnp.bfloat16)
    d_mixed[...] = nn_dot(d_attn, w_out[...]).astype(jnp.bfloat16)
    for j in range(2):
        up = tn_dot(d_proj[:, FF * j : FF * (j + 1)], a2)
        put_both(place, send, keep, 0, up, everyone[8 * j : 8 * j + 8])
    put_both(place, send, keep, 144, tn_dot(d_attn, mixed[...]), everyone)
    down_grad = tn_dot(out_grad, hidden[...])
    put_both(place, send, keep, 192, down_grad, everyone)
    rest = down_grad[:, 2 * HALF :]
    for chip in everyone:
        put_rows(place, send, keep, 0, 240, rest[48 * chip : 48 * chip + 32], [chip])
        put_rows(place, send, keep, 1, 240, rest[48 * chip + 32 : 48 * chip + 48], [chip])
        put_rows(place, send, keep, 1, 256, gain_rows(gain_grad, chip), [chip])


def attend_back_kernel(
    place, query, pairs, before, after, bias, d_mixed,
    d_query, d_own, rim_before, rim_after, framed, d_framed,
):
    frame_pairs(place, pairs, before, after, framed)
    is_low, low, high = head_masks()
    d_framed[256:SPAN, :] = jnp.zeros((SPAN - 256, 2 * D), jnp.float32)
    scale = 1.0 / math.sqrt(HD)
    for block in range(2):
        rows, keys = slice(128 * block, 128 * block + 128), slice(128 * block, 128 * block + 256)
        both = jnp.concatenate([bias[rows, :], bias[rows, :]], axis=0)
        for p in range(PAIRS):
            lanes, vlanes = slice(PAIR * p, PAIR * (p + 1)), slice(D + PAIR * p, D + PAIR * (p + 1))
            q2 = stack_heads(query[rows, lanes], low, high)
            o2 = stack_heads(d_mixed[rows, lanes], low, high)
            k2 = framed[keys, lanes]
            probs = probabilities(q2, k2, both)
            d_probs = nt_dot(o2, framed[keys, vlanes])
            spread = jnp.sum(probs * d_probs, axis=-1, keepdims=True)
            d_scores = (probs * (d_probs - spread)).astype(jnp.bfloat16)
            d_q = nn_dot(d_scores, k2) * scale
            d_query[rows, lanes] = jnp.where(is_low, d_q[:128], d_q[128:])
            d_k = tn_dot(d_scores, q2) * scale
            d_v = tn_dot(probs.astype(jnp.bfloat16), o2)
            if block == 0:
                d_framed[keys, lanes] = d_k
                d_framed[keys, vlanes] = d_v
            else:
                d_framed[keys, lanes] += d_k
                d_framed[keys, vlanes] += d_v
    rim_before[...] = d_framed[0:WIN, :].astype(jnp.bfloat16)
    tail = pl.ds(pl.multiple_of(WIN + place[AT_LIVE], 64), WIN)
    rim_after[...] = d_framed[tail, :].astype(jnp.bfloat16)
    d_own[...] = d_framed[WIN : WIN + SLOTS, :]


def finish_kernel(
    place, tokens, first, gain, weight, d_query, d_own, from_before, from_after, cos, sin_a, sin_b, d_after,
    tokens_grad, send, keep, d_joined, d_pairs,
):
    live = lax.broadcasted_iota(jnp.int32, (SLOTS, 1), 0) < place[AT_LIVE]
    d_pairs[...] = jnp.where(live, d_own[...], 0.0)
    d_pairs[0:WIN, :] += from_before[...].astype(jnp.float32)
    tail = pl.ds(pl.multiple_of(place[AT_LIVE] - WIN, 64), WIN)
    d_pairs[tail, :] += from_after[...].astype(jnp.float32)
    c, sa, sb = cos[...], sin_a[...], sin_b[...]
    for part in range(2):
        source = d_query if part == 0 else d_pairs
        for p in range(PAIRS):
            v = source[:, PAIR * p : PAIR * (p + 1)]
            v = v * c - pltpu.roll(v, 96, 1) * sa - pltpu.roll(v, 32, 1) * sb
            d_joined[:, part * D + PAIR * p : part * D + PAIR * (p + 1)] = v.astype(jnp.bfloat16)
    d_joined[:, 2 * D :] = d_pairs[:, D:].astype(jnp.bfloat16)
    d_first = nn_dot(d_joined[...], weight[...])
    normed, factor = norm_parts(tokens[...].astype(jnp.float32))
    gain_grad = jnp.sum(normed * d_first, axis=0, keepdims=True)
    d_stream = d_after[...] + norm_back(d_first * gain[...], normed, factor)
    tokens_grad[...] = jnp.where(live, d_stream, 0.0)
    everyone = list(range(CHIPS))
    for j in range(2):
        up = tn_dot(d_joined[:, 1152 * j : 1152 * (j + 1)], first[...])
        put_both(place, send, keep, 0, up, everyone[8 * j : 8 * j + 8])
    for chip in everyone:
        for stream in (0, 1):
            put_rows(place, send, keep, stream, 144, gain_rows(gain_grad, chip), [chip])


def swap_halves(shard, core, sibling):
    low, high = shard[:, :HALF], shard[:, HALF:]
    own = jnp.where(core == 0, low, high)
    return own, permute(jnp.where(core == 0, high, low), sibling)


def interleave(own, got, core, cuts):
    parts, start = [], 0
    for count in cuts:
        mine, theirs = own[start : start + count], got[start : start + count]
        parts += [jnp.where(core == 0, mine, theirs), jnp.where(core == 0, theirs, mine)]
        start += count
    return parts


def spread_line(block, line):
    return jnp.stack([block] + [permute(block, line[k]) for k in (1, 2, 3)])


def reduce_near(send, keep, links_of):
    return keep + permute(send, links_of[0])


def sum_shares(own, others):
    share = own.astype(jnp.float32)
    for other in others:
        share = share + other.astype(jnp.float32)
    return share


def place_table(live_rows):
    z, y, x, core = chip_place()
    slots = jnp.arange(CHIPS, dtype=jnp.int32)
    zr, nr, fr = slots % 4, slots // 4 % 2, slots // 8
    held = []
    for own in (True, False):
        along_y = (core == 0) if own else (core == 1)
        yr, xr = jnp.where(along_y, nr, fr), jnp.where(along_y, fr, nr)
        held.append((z - zr) % 4 * 4 + (y ^ yr) * 2 + (x ^ xr))
    zz, yy, xx = slots // 4, slots // 2 % 2, slots % 2
    yr, xr = y ^ yy, x ^ xx
    put = []
    for n, f in ((yr, xr), (xr, yr)):
        put.append((1 - n) * 8 + (1 - f) * 4 + (zz - z + 3) % 4)
    head = jnp.stack([live_rows, core]).astype(jnp.int32)
    return jnp.concatenate([head] + held + put).astype(jnp.int32)


def fused_body(
    tokens, w_qkv, w_out, w_up, w_down, gain_attn, gain_mlp, cotangent, block_counts, seq_lengths
):
    bf16, f32 = jnp.bfloat16, jnp.float32
    device_index = lax.axis_index("fsdp")
    core = device_index % 2
    wires = links()
    sibling, near, far, line = wires
    gains = jnp.zeros((8, D), bf16)
    gain_pair = jnp.pad(jnp.stack([gain_attn, gain_mlp]), ((0, 6), (0, HALF - 24)))
    gains = jnp.concatenate([gain_pair, gain_pair], axis=1)
    own, got = swap_halves(jnp.concatenate([w_qkv.T, gains]), core, sibling)
    block = jnp.concatenate(interleave(own, got, core, (72, 8)))
    lined_one = spread_line(block, line)
    near_one, far_one = permute(lined_one, near), permute(lined_one, far)
    both_one = permute(near_one, far)
    mine_one = [lined_one, near_one, far_one, both_one]
    blocks_one = mine_one + [permute(piece, sibling) for piece in mine_one]
    block_counts, seq_lengths, _ = lax.optimization_barrier((block_counts, seq_lengths, lined_one))
    block_count = lax.dynamic_index_in_dim(block_counts, device_index, keepdims=False)
    device_ids = jnp.arange(block_counts.shape[0], dtype=jnp.int32)
    first_place = jnp.sum(jnp.where(device_ids < device_index, block_counts, 0)) * BLK
    live_rows = block_count * BLK
    stream_total = jnp.sum(block_counts) * BLK
    place = place_table(live_rows)
    slot_index = jnp.arange(SLOTS, dtype=jnp.int32)
    live_slots = slot_index < live_rows
    query_place = first_place + slot_index
    query_seg, query_pos = sequence_places(query_place, seq_lengths)
    key_slot = (slot_index // BLK * BLK)[:, None] + jnp.arange(256, dtype=jnp.int32)[None, :] - WIN
    key_place = first_place + key_slot
    ends = jnp.cumsum(seq_lengths)
    key_seg = jnp.sum((key_place[:, :, None] >= ends).astype(jnp.int32), axis=2)
    allowed = (
        live_slots[:, None]
        & (key_place >= 0)
        & (key_place < stream_total)
        & (query_seg[:, None] == key_seg)
        & (jnp.abs(query_place[:, None] - key_place) <= WIN)
    ) | (jnp.logical_not(live_slots)[:, None] & (key_slot == slot_index[:, None]))
    bias = jnp.where(allowed, 0.0, MASKED).astype(f32)
    cosine, sine = rotary_tables(query_pos)
    cosine, sine = (jnp.concatenate([t[:, 0], t[:, 0]], axis=1) for t in (cosine, sine))
    front = (jnp.arange(PAIR) % HD < HD // 2)[None, :]
    sin_a, sin_b = jnp.where(front, -sine, 0.0), jnp.where(front, 0.0, sine)
    chosen = (place[AT_CHIP : AT_CHIP + 16][None, :] == jnp.arange(CHIPS)[:, None]).astype(f32)
    flat = jnp.concatenate([piece[:, 144:, :24] for piece in mine_one]).astype(f32)
    flat = jnp.concatenate([flat[:, row] for row in (0, 8, 1, 9)], axis=1)
    flat = jnp.sum(chosen[:, :, None] * flat[None], axis=1)
    gain_a, gain_m = flat[:, :48].reshape(1, D), flat[:, 48:].reshape(1, D)
    query, pairs, first, weight = call(
        project_kernel,
        [((SLOTS, D), bf16), ((SLOTS, 2 * D), bf16), ((SLOTS, D), bf16), ((3 * D, D), bf16)],
        [],
        [place, tokens, gain_a, cosine, sin_a, sin_b] + blocks_one,
        6,
        8,
    )
    shard = jnp.concatenate([w_up.T, w_out.T, w_down.T[:, :D]])
    rest = w_down.T[:, D:]
    low, high = shard[:, :HALF], shard[:, HALF:]
    own = jnp.concatenate([jnp.where(core == 0, low, high), rest[:8]])
    got = permute(jnp.concatenate([jnp.where(core == 0, high, low), rest[:8]]), sibling)
    tail = jnp.where(
        core == 0,
        jnp.concatenate([rest, got[120:128]]),
        jnp.concatenate([rest[8:], jnp.zeros((16, HALF), bf16)]),
    )
    block = jnp.concatenate(interleave(own, got, core, (72, 24, 24)) + [tail])
    block, _ = lax.optimization_barrier((block, lined_one))
    lined_two, _ = lax.optimization_barrier((spread_line(block, line), both_one))
    near_two, far_two = permute(lined_two, near), permute(lined_two, far)
    up = [(i, i + 1) for i in range(31)]
    down = [(i + 1, i) for i in range(31)]
    before = permute(lax.dynamic_slice_in_dim(pairs, live_rows - WIN, WIN, 0), up)
    after = permute(pairs[:WIN], down)
    near_two, pairs = lax.optimization_barrier((near_two, pairs))
    both_two = permute(near_two, far)
    (mixed,) = call(
        attend_kernel,
        [((SLOTS, D), bf16)],
        [((SPAN, 2 * D), bf16)],
        [place, query, pairs, before, after, bias],
        3,
    )
    mine_two = [lined_two, near_two, far_two]
    other_two = [permute(piece, sibling) for piece in mine_two]
    both_two, mixed = lax.optimization_barrier((both_two, mixed))
    blocks_two = mine_two + [both_two] + other_two + [permute(both_two, sibling)]
    block_out, d_after, d_mixed, send, keep = call(
        middle_kernel,
        [((SLOTS, D), bf16), ((SLOTS, D), f32), ((SLOTS, D), bf16), ((CHIPS, ROWS2, HALF), bf16), ((CHIPS, ROWS2, HALF), bf16)],
        [((2 * FF, D), bf16), ((D, D), bf16), ((D, FF), bf16), ((SLOTS, 2 * FF), bf16), ((SLOTS, FF), bf16)],
        [place, tokens, mixed, gain_m, cotangent] + blocks_two,
        14,
        8,
    )
    d_query, d_own, rim_before, rim_after = call(
        attend_back_kernel,
        [((SLOTS, D), f32), ((SLOTS, 2 * D), f32), ((WIN, 2 * D), bf16), ((WIN, 2 * D), bf16)],
        [((SPAN, 2 * D), bf16), ((SPAN, 2 * D), f32)],
        [place, query, pairs, before, after, bias, d_mixed],
        8,
    )
    from_after = permute(rim_before, down)
    from_before = permute(rim_after, up)
    total = reduce_near(send, keep, wires)
    leaving, staying = total[:8], total[8:]
    leaving, from_after, from_before = lax.optimization_barrier((leaving, from_after, from_before))
    arrived = permute(leaving, near)
    tokens_grad, send_qkv, keep_qkv = call(
        finish_kernel,
        [((SLOTS, D), f32), ((CHIPS, ROWS1, HALF), bf16), ((CHIPS, ROWS1, HALF), bf16)],
        [((SLOTS, 3 * D), bf16), ((SLOTS, 2 * D), f32)],
        [place, tokens, first, gain_a, weight, d_query, d_own, from_before, from_after, cosine, sin_a, sin_b, d_after],
        9,
    )
    total = staying + arrived
    total, send_qkv, keep_qkv = lax.optimization_barrier((total, send_qkv, keep_qkv))
    leaving, staying = total[:4], total[4:]
    arrived = permute(leaving, far)
    total_qkv = reduce_near(send_qkv, keep_qkv, wires)
    leave_qkv, stay_qkv = total_qkv[:8], total_qkv[8:]
    arrived_qkv = permute(leave_qkv, near)
    staying, stay_qkv = lax.optimization_barrier((staying, stay_qkv))
    total = staying + arrived
    last = [permute(total[k], line[k + 1]) for k in range(3)]
    stay_qkv, last[0] = lax.optimization_barrier((stay_qkv, last[0]))
    total_qkv = stay_qkv + arrived_qkv
    arrived_qkv = permute(total_qkv[:4], far)
    total_qkv = total_qkv[4:] + arrived_qkv
    share, total_qkv = lax.optimization_barrier((total[3], total_qkv))
    share = sum_shares(share, last)
    last_qkv = [permute(total_qkv[k], line[k + 1]) for k in range(3)]
    chip = device_index // 2
    lane = 48 * chip - jnp.minimum(48 * chip // 128 * 128, D - HALF) + 24 * core

    def part(block, start, count, whose):
        return lax.dynamic_slice_in_dim(block, start + count * whose, count, 0)

    gain_row = lax.dynamic_slice_in_dim(share[256:264], lane - 24 * core, 48, 1)
    gain_row = jnp.pad(gain_row, ((0, 0), (0, HALF - 48)))
    cuts = ((0, 72), (144, 24), (192, 24))
    theirs = jnp.concatenate(
        [part(share, s, n, 1 - core) for s, n in cuts] + [jnp.where(core == 0, share[264:272], gain_row)]
    )
    own = jnp.concatenate([part(share, s, n, core) for s, n in cuts])
    got = permute(theirs, sibling)
    both = jnp.concatenate(
        [jnp.where(core == 0, own, got[:120]), jnp.where(core == 0, got[:120], own)], axis=1
    )
    last = jnp.where(
        core == 0, share[240:264], jnp.concatenate([got[120:128], share[240:256]])
    )
    up_sum, out_sum = both[:72].T, both[72:96].T
    down_sum = jnp.concatenate([both[96:], last], axis=1).T
    gain_m_sum = jnp.where(core == 0, got[120, :24], gain_row[0, 24:48])
    share = sum_shares(total_qkv[3], last_qkv)
    got = permute(part(share, 0, 72, 1 - core), sibling)
    own = part(share, 0, 72, core)
    qkv_sum = jnp.concatenate([jnp.where(core == 0, own, got), jnp.where(core == 0, got, own)], axis=1).T
    gain_a_sum = lax.dynamic_slice(share, (144, lane), (1, 24))[0]
    return (block_out, tokens_grad, qkv_sum, out_sum, up_sum, down_sum, gain_a_sum, gain_m_sum)


def solution(mesh):
    plan = fused_body if mesh.shape["fsdp"] == 32 else body
    placed = (
        P("fsdp", None),
        P(None, "fsdp"),
        P(None, "fsdp"),
        P(None, "fsdp"),
        P(None, "fsdp"),
        P("fsdp"),
        P("fsdp"),
        P("fsdp", None),
        P(),
        P(),
    )
    return jax.shard_map(
        plan,
        mesh=mesh,
        in_specs=placed,
        out_specs=(
            P("fsdp", None),
            P("fsdp", None),
            P(None, "fsdp"),
            P(None, "fsdp"),
            P(None, "fsdp"),
            P(None, "fsdp"),
            P("fsdp"),
            P("fsdp"),
        ),
        check_vma=False,
    )
```

profile of v0, /device:TPU:13, one launch (start us, length us, event | category | flops | bytes accessed | tf_op | source)
XLA Modules:
  0.0 201.6 jit_solution(5143876947069392492)
XLA Ops:
  11.7 7.0 %collective-permute-done.2 = bf16[160,384]{1,0:T(8,128)(2,1)S(1)} collective-permute-done((bf16[160,384]{1,0:T(8,128)(2,1)S(1)}, bf16[160,384]{1,0:T(8,128)(2,1)S(1)}, u32[]{:S(2)}, u32[]{:S(2)}) %collective-permute-start.2) | collective-permute-done | bytes 122912 | tf_op jit(solution)/shard_map/ppermute | solution.py:107
  18.7 2.5 %collective-permute-done.3 = bf16[160,384]{1,0:T(8,128)(2,1)S(1)} collective-permute-done((bf16[160,384]{1,0:T(8,128)(2,1)S(1)}, bf16[160,384]{1,0:T(8,128)(2,1)S(1)}, u32[]{:S(2)}, u32[]{:S(2)}) %collective-permute-start.3) | collective-permute-done | bytes 122912 | tf_op jit(solution)/shard_map/ppermute | solution.py:107
  27.4 5.9 %collective-permute-done.8.rest_1_ = bf16[4,160,384]{2,1,0:T(8,128)(2,1)S(1)} collective-permute-done((bf16[4,160,384]{2,1,0:T(8,128)(2,1)S(1)}, bf16[4,160,384]{2,1,0:T(8,128)(2,1)S(1)}, u32[]{:S(2)}, u32[]{:S(2)}) %collective-permute-start.8) | collective-permute-done | bytes 491552 | tf_op jit(solution)/shard_map/ppermute | solution.py:107
  35.8 3.6 %collective-permute-start.12 = (bf16[4,160,384]{2,1,0:T(8,128)(2,1)S(1)}, bf16[4,160,384]{2,1,0:T(8,128)(2,1)}, u32[]{:S(2)}, u32[]{:S(2)}) collective-permute-start(bf16[4,160,384]{2,1,0:T(8,128)(2,1)S(1)} %pad_maximum_fusion.1.rest_0_), channel_id=1, source_target_pairs={{0,1},{1,0},{2,3},{3,2},{4,5},{5,4},{6,7},{7,6},{8,9},{9,8},{10,11... | collective-permute-start | bytes 1474568 | tf_op jit(solution)/shard_map/ppermute | solution.py:107
  40.0 2.6 %collective-permute-done.7 = bf16[272,384]{1,0:T(8,128)(2,1)} collective-permute-done((bf16[272,384]{1,0:T(8,128)(2,1)S(1)}, bf16[272,384]{1,0:T(8,128)(2,1)}, u32[]{:S(2)}, u32[]{:S(2)}) %collective-permute-start.7) | collective-permute-done | bytes 208928 | tf_op jit(solution)/shard_map/ppermute | solution.py:107
  46.0 1.8 collective-permute-start.13
  52.7 6.8 %shard_map.161 = (bf16[256,768]{1,0:T(8,128)(2,1)S(1)}, bf16[256,1536]{1,0:T(8,128)(2,1)}, bf16[256,768]{1,0:T(8,128)(2,1)S(1)}, bf16[2304,768]{1,0:T(8,128)(2,1)}) custom-call(s32[66]{0:T(128)S(1)} %concatenate.67.place, bf16[256,768]{1,0:T(8,128)(2,1)S(1)} %copy-done.1, f32[1,768]{1,0:T(1,128)S(1)} %reshape.219.gain, ...), custom_call_target="tpu_custom_call" | custom-call | bytes 22140000 | tf_op jit(solution)/shard_map/pallas_call | solution.py:328
  61.4 4.4 %collective-permute-start.17 = (bf16[64,1536]{1,0:T(8,128)(2,1)S(1)}, bf16[64,1536]{1,0:T(8,128)(2,1)S(1)}, u32[]{:S(2)}, u32[]{:S(2)}) collective-permute-start(bf16[64,1536]{1,0:T(8,128)(2,1)S(1)} %get-tuple-element.91), channel_id=1, source_target_pairs={{0,1},{1,2},{2,3},{3,4},{4,5},{5,6},{6,7},{7,8},{8,9},{9,10},{10,1... | collective-permute-start | bytes 589832 | tf_op jit(solution)/shard_map/ppermute | solution.py:107
  65.8 1.9 collective-permute-start.18
  68.0 2.6 %collective-permute-start.20 = (bf16[4,272,384]{2,1,0:T(8,128)(2,1)S(1)}, bf16[4,272,384]{2,1,0:T(8,128)(2,1)}, u32[]{:S(2)}, u32[]{:S(2)}) collective-permute-start(bf16[4,272,384]{2,1,0:T(8,128)(2,1)S(1)} %pad_maximum_fusion.rest_0_), channel_id=1, source_target_pairs={{0,1},{1,0},{2,3},{3,2},{4,5},{5,4},{6,7},{7,6},{8,9},{9,8},{10,11... | collective-permute-start | bytes 2506760 | tf_op jit(solution)/shard_map/ppermute | solution.py:107
  70.7 3.2 %collective-permute-start.21 = (bf16[4,272,384]{2,1,0:T(8,128)(2,1)}, bf16[4,272,384]{2,1,0:T(8,128)(2,1)}, u32[]{:S(2)}, u32[]{:S(2)}) collective-permute-start(bf16[4,272,384]{2,1,0:T(8,128)(2,1)} %collective-permute-done.10.rest_1_), channel_id=1, source_target_pairs={{0,1},{1,0},{2,3},{3,2},{4,5},{5,4},{6,7},{7,6},{8,9},{9,8},{10,11... | collective-permute-start | bytes 2506760 | tf_op jit(solution)/shard_map/ppermute | solution.py:107
  73.9 3.5 %collective-permute-done.18.after = bf16[64,1536]{1,0:T(8,128)(2,1)S(1)} collective-permute-done((bf16[64,1536]{1,0:T(8,128)(2,1)S(1)}, bf16[64,1536]{1,0:T(8,128)(2,1)S(1)}, u32[]{:S(2)}, u32[]{:S(2)}) %collective-permute-start.18) | collective-permute-done | bytes 196640 | tf_op jit(solution)/shard_map/ppermute | solution.py:107
  77.4 2.6 %shard_map.162.mixed = bf16[256,768]{1,0:T(8,128)(2,1)S(1)} custom-call(s32[66]{0:T(128)S(1)} %concatenate.67.place, bf16[256,768]{1,0:T(8,128)(2,1)S(1)} %get-tuple-element.50.query, bf16[256,1536]{1,0:T(8,128)(2,1)S(1)} %copy-done, bf16[64,1536]{1,0:T(8,128)(2,1)S(1)} %collective-permute-done.17.before, ...), custom_call_target="tpu_custom_call" | custom-call | bytes 11070000 | tf_op jit(solution)/shard_map/pallas_call | solution.py:328
  80.9 2.6 %collective-permute-done.23.rest_7_ = bf16[4,272,384]{2,1,0:T(8,128)(2,1)} collective-permute-done((bf16[4,272,384]{2,1,0:T(8,128)(2,1)}, bf16[4,272,384]{2,1,0:T(8,128)(2,1)}, u32[]{:S(2)}, u32[]{:S(2)}) %collective-permute-start.23) | collective-permute-done | bytes 835616 | tf_op jit(solution)/shard_map/ppermute | solution.py:107
  84.4 16.8 %shard_map.163 = (bf16[256,768]{1,0:T(8,128)(2,1)}, f32[256,768]{1,0:T(8,128)S(1)}, bf16[256,768]{1,0:T(8,128)(2,1)S(1)}, bf16[16,272,384]{2,1,0:T(8,128)(2,1)}, bf16[16,272,384]{2,1,0:T(8,128)(2,1)}) custom-call(s32[66]{0:T(128)S(1)} %concatenate.67.place, bf16[256,768]{1,0:T(8,128)(2,1)S(1)} %copy-done.1, bf16[256,768]{1,0:T(8,128)(2,1)S(1)} %shard_map.162.mixed, ...), custom_call_target="tpu_custom_call" | custom-call | bytes 51660000 | tf_op jit(solution)/shard_map/pallas_call | solution.py:328
  101.4 7.4 %shard_map.164 = (f32[256,768]{1,0:T(8,128)S(1)}, f32[256,1536]{1,0:T(8,128)S(1)}, bf16[64,1536]{1,0:T(8,128)(2,1)S(1)}, bf16[64,1536]{1,0:T(8,128)(2,1)S(1)}) custom-call(s32[66]{0:T(128)S(1)} %concatenate.67.place, bf16[256,768]{1,0:T(8,128)(2,1)S(1)} %get-tuple-element.50.query, bf16[256,1536]{1,0:T(8,128)(2,1)S(1)} %copy-done, ...), custom_call_target="tpu_custom_call" | custom-call | bytes 29520000 | tf_op jit(solution)/shard_map/pallas_call | solution.py:328
  108.8 2.3 %collective-permute-start.25 = (bf16[64,1536]{1,0:T(8,128)(2,1)S(1)}, bf16[64,1536]{1,0:T(8,128)(2,1)S(1)}, u32[]{:S(2)}, u32[]{:S(2)}) collective-permute-start(bf16[64,1536]{1,0:T(8,128)(2,1)S(1)} %get-tuple-element.62), channel_id=1, source_target_pairs={{1,0},{2,1},{3,2},{4,3},{5,4},{6,5},{7,6},{8,7},{9,8},{10,9},{11,1... | collective-permute-start | bytes 589832 | tf_op jit(solution)/shard_map/ppermute | solution.py:107
  111.1 3.2 %collective-permute-start.26 = (bf16[64,1536]{1,0:T(8,128)(2,1)S(1)}, bf16[64,1536]{1,0:T(8,128)(2,1)S(1)}, u32[]{:S(2)}, u32[]{:S(2)}) collective-permute-start(bf16[64,1536]{1,0:T(8,128)(2,1)S(1)} %get-tuple-element.63), channel_id=1, source_target_pairs={{0,1},{1,2},{2,3},{3,4},{4,5},{5,6},{6,7},{7,8},{8,9},{9,10},{10,1... | collective-permute-start | bytes 589832 | tf_op jit(solution)/shard_map/ppermute | solution.py:107
  114.4 2.9 %add.311 = bf16[16,272,384]{2,1,0:T(8,128)(2,1)S(1)} add(bf16[16,272,384]{2,1,0:T(8,128)(2,1)} %get-tuple-element.60, bf16[16,272,384]{2,1,0:T(8,128)(2,1)S(1)} %collective-permute-done.24) | non-fusion elementwise | flops 1671168 | bytes 10027008 | tf_op jit(solution)/shard_map/add | solution.py:603
  119.1 8.9 %shard_map.165 = (f32[256,768]{1,0:T(8,128)}, bf16[16,160,384]{2,1,0:T(8,128)(2,1)}, bf16[16,160,384]{2,1,0:T(8,128)(2,1)}) custom-call(s32[66]{0:T(128)S(1)} %concatenate.67.place, bf16[256,768]{1,0:T(8,128)(2,1)S(1)} %copy-done.1, bf16[256,768]{1,0:T(8,128)(2,1)S(1)} %copy-done.10, f32[1,768]{1,0:T(1,128)S(1)} %reshape.219.gain, ...), custom_call_target="tpu_custom_call" | custom-call | bytes 33210000 | tf_op jit(solution)/shard_map/pallas_call | solution.py:328
  128.1 10.6 %collective-permute-done.27 = bf16[8,272,384]{2,1,0:T(8,128)(2,1)S(1)} collective-permute-done((bf16[8,272,384]{2,1,0:T(8,128)(2,1)S(1)}, bf16[8,272,384]{2,1,0:T(8,128)(2,1)S(1)}, u32[]{:S(2)}, u32[]{:S(2)}) %collective-permute-start.27) | collective-permute-done | bytes 1671200 | tf_op jit(solution)/shard_map/ppermute | solution.py:107
  138.9 3.9 %collective-permute-start.28 = (bf16[16,160,384]{2,1,0:T(8,128)(2,1)S(1)}, bf16[16,160,384]{2,1,0:T(8,128)(2,1)S(1)}, u32[]{:S(2)}, u32[]{:S(2)}) collective-permute-start(bf16[16,160,384]{2,1,0:T(8,128)(2,1)S(1)} %copy-done.14), channel_id=1, source_target_pairs={{0,1},{1,0},{2,3},{3,2},{4,5},{5,4},{6,7},{7,6},{8,9},{9,8},{10,11... | collective-permute-start | bytes 5898248 | tf_op jit(solution)/shard_map/ppermute | solution.py:107
  143.1 3.3 %collective-permute-done.28 = bf16[16,160,384]{2,1,0:T(8,128)(2,1)S(1)} collective-permute-done((bf16[16,160,384]{2,1,0:T(8,128)(2,1)S(1)}, bf16[16,160,384]{2,1,0:T(8,128)(2,1)S(1)}, u32[]{:S(2)}, u32[]{:S(2)}) %collective-permute-start.28) | collective-permute-done | bytes 1966112 | tf_op jit(solution)/shard_map/ppermute | solution.py:107
  147.3 11.3 %collective-permute-done.29 = bf16[4,272,384]{2,1,0:T(8,128)(2,1)S(1)} collective-permute-done((bf16[4,272,384]{2,1,0:T(8,128)(2,1)S(1)}, bf16[4,272,384]{2,1,0:T(8,128)(2,1)S(1)}, u32[]{:S(2)}, u32[]{:S(2)}) %collective-permute-start.29) | collective-permute-done | bytes 835616 | tf_op jit(solution)/shard_map/ppermute | solution.py:107
  158.9 4.9 %collective-permute-done.30 = bf16[272,384]{1,0:T(8,128)(2,1)S(1)} collective-permute-done((bf16[272,384]{1,0:T(8,128)(2,1)S(1)}, bf16[272,384]{1,0:T(8,128)(2,1)S(1)}, u32[]{:S(2)}, u32[]{:S(2)}) %collective-permute-start.30) | collective-permute-done | bytes 208928 | tf_op jit(solution)/shard_map/ppermute | solution.py:107
  163.9 1.9 collective-permute-done.31
  166.2 1.9 collective-permute-start.37
  168.3 5.8 %collective-permute-done.32 = bf16[4,160,384]{2,1,0:T(8,128)(2,1)S(1)} collective-permute-done((bf16[4,160,384]{2,1,0:T(8,128)(2,1)S(1)}, bf16[4,160,384]{2,1,0:T(8,128)(2,1)S(1)}, u32[]{:S(2)}, u32[]{:S(2)}) %collective-permute-start.32) | collective-permute-done | bytes 491552 | tf_op jit(solution)/shard_map/ppermute | solution.py:107
  174.1 7.8 %collective-permute-done.37 = bf16[272,384]{1,0:T(8,128)(2,1)S(1)} collective-permute-done((bf16[272,384]{1,0:T(8,128)(2,1)S(1)}, bf16[272,384]{1,0:T(8,128)(2,1)S(1)}, u32[]{:S(2)}, u32[]{:S(2)}) %collective-permute-start.37) | collective-permute-done | bytes 208928 | tf_op jit(solution)/shard_map/ppermute | solution.py:107
  182.2 3.2 %collective-permute-start.34 = (bf16[160,384]{1,0:T(8,128)(2,1)S(1)}, bf16[160,384]{1,0:T(8,128)(2,1)S(1)}, u32[]{:S(2)}, u32[]{:S(2)}) collective-permute-start(bf16[160,384]{1,0:T(8,128)(2,1)S(1)} %get-tuple-element.94), channel_id=1, source_target_pairs={{0,16},{1,17},{2,18},{3,19},{4,20},{5,21},{6,22},{7,23},{8,24},{9,... | collective-permute-start | bytes 368648 | tf_op jit(solution)/shard_map/ppermute | solution.py:107
  188.2 4.6 %collective-permute-done.34 = bf16[160,384]{1,0:T(8,128)(2,1)S(1)} collective-permute-done((bf16[160,384]{1,0:T(8,128)(2,1)S(1)}, bf16[160,384]{1,0:T(8,128)(2,1)S(1)}, u32[]{:S(2)}, u32[]{:S(2)}) %collective-permute-start.34) | collective-permute-done | bytes 122912 | tf_op jit(solution)/shard_map/ppermute | solution.py:107
  192.8 4.2 %collective-permute-done.35 = bf16[160,384]{1,0:T(8,128)(2,1)S(1)} collective-permute-done((bf16[160,384]{1,0:T(8,128)(2,1)S(1)}, bf16[160,384]{1,0:T(8,128)(2,1)S(1)}, u32[]{:S(2)}, u32[]{:S(2)}) %collective-permute-start.35) | collective-permute-done | bytes 122912 | tf_op jit(solution)/shard_map/ppermute | solution.py:107
  (173 shorter events, 42.4 us)
Async XLA Ops:
  5.5 5.6 %collective-permute-start.4 = (bf16[128,384]{1,0:T(8,128)(2,1)S(1)}, bf16[128,384]{1,0:T(8,128)(2,1)S(1)}, u32[]{:S(2)}, u32[]{:S(2)}) collective-permute-start(bf16[128,384]{1,0:T(8,128)(2,1)S(1)} %pad_maximum_fusion.10), channel_id=1, source_target_pairs={{0,1},{1,0},{2,3},{3,2},{4,5},{5,4},{6,7},{7,6},{8,9},{9,8},{10,11... | collective-permute-start | bytes 294920 | tf_op jit(solution)/shard_map/ppermute | solution.py:107
  8.6 10.2 %collective-permute-start.2 = (bf16[160,384]{1,0:T(8,128)(2,1)S(1)}, bf16[160,384]{1,0:T(8,128)(2,1)S(1)}, u32[]{:S(2)}, u32[]{:S(2)}) collective-permute-start(bf16[160,384]{1,0:T(8,128)(2,1)S(1)} %get-tuple-element.113), channel_id=1, source_target_pairs={{0,16},{1,17},{2,18},{3,19},{4,20},{5,21},{6,22},{7,23},{8,24},{9,... | collective-permute-start | bytes 368648 | tf_op jit(solution)/shard_map/ppermute | solution.py:107
  9.7 11.6 %collective-permute-start.3 = (bf16[160,384]{1,0:T(8,128)(2,1)S(1)}, bf16[160,384]{1,0:T(8,128)(2,1)S(1)}, u32[]{:S(2)}, u32[]{:S(2)}) collective-permute-start(bf16[160,384]{1,0:T(8,128)(2,1)S(1)} %get-tuple-element.113), channel_id=1, source_target_pairs={{0,24},{1,25},{2,26},{3,27},{4,28},{5,29},{6,30},{7,31},{8,0},{9,1... | collective-permute-start | bytes 368648 | tf_op jit(solution)/shard_map/ppermute | solution.py:107
  21.4 11.9 %collective-permute-start.8 = (bf16[4,160,384]{2,1,0:T(8,128)(2,1)S(1)}, bf16[4,160,384]{2,1,0:T(8,128)(2,1)S(1)}, u32[]{:S(2)}, u32[]{:S(2)}) collective-permute-start(bf16[4,160,384]{2,1,0:T(8,128)(2,1)S(1)} %pad_maximum_fusion.1.rest_0_), channel_id=1, source_target_pairs={{0,4},{1,3},{2,6},{3,1},{4,0},{5,7},{6,2},{7,5},{8,12},{9,11},{10,... | collective-permute-start | bytes 1474568 | tf_op jit(solution)/shard_map/ppermute | solution.py:107
  22.6 25.2 %collective-permute-start.11 = (bf16[4,160,384]{2,1,0:T(8,128)(2,1)S(1)}, bf16[4,160,384]{2,1,0:T(8,128)(2,1)S(1)}, u32[]{:S(2)}, u32[]{:S(2)}) collective-permute-start(bf16[4,160,384]{2,1,0:T(8,128)(2,1)S(1)} %pad_maximum_fusion.1.rest_0_), channel_id=1, source_target_pairs={{0,2},{1,5},{2,0},{3,7},{4,6},{5,1},{6,4},{7,3},{8,10},{9,13},{10,... | collective-permute-start | bytes 1474568 | tf_op jit(solution)/shard_map/ppermute | solution.py:107
  22.9 12.9 %collective-permute-start.5 = (bf16[272,384]{1,0:T(8,128)(2,1)S(1)}, bf16[272,384]{1,0:T(8,128)(2,1)S(1)}, u32[]{:S(2)}, u32[]{:S(2)}) collective-permute-start(bf16[272,384]{1,0:T(8,128)(2,1)S(1)} %fusion.14), channel_id=1, source_target_pairs={{0,8},{1,9},{2,10},{3,11},{4,12},{5,13},{6,14},{7,15},{8,16},{9,17... | collective-permute-start | bytes 626696 | tf_op jit(solution)/shard_map/ppermute | solution.py:107
  22.9 17.1 %collective-permute-start.6 = (bf16[272,384]{1,0:T(8,128)(2,1)S(1)}, bf16[272,384]{1,0:T(8,128)(2,1)}, u32[]{:S(2)}, u32[]{:S(2)}) collective-permute-start(bf16[272,384]{1,0:T(8,128)(2,1)S(1)} %fusion.14), channel_id=1, source_target_pairs={{0,16},{1,17},{2,18},{3,19},{4,20},{5,21},{6,22},{7,23},{8,24},{9,... | collective-permute-start | bytes 626696 | tf_op jit(solution)/shard_map/ppermute | solution.py:107
  23.5 19.2 %collective-permute-start.7 = (bf16[272,384]{1,0:T(8,128)(2,1)S(1)}, bf16[272,384]{1,0:T(8,128)(2,1)}, u32[]{:S(2)}, u32[]{:S(2)}) collective-permute-start(bf16[272,384]{1,0:T(8,128)(2,1)S(1)} %fusion.14), channel_id=1, source_target_pairs={{0,24},{1,25},{2,26},{3,27},{4,28},{5,29},{6,30},{7,31},{8,0},{9,1... | collective-permute-start | bytes 626696 | tf_op jit(solution)/shard_map/ppermute | solution.py:107
  33.2 10.6 %collective-permute-start.9 = (bf16[4,160,384]{2,1,0:T(8,128)(2,1)S(1)}, bf16[4,160,384]{2,1,0:T(8,128)(2,1)}, u32[]{:S(2)}, u32[]{:S(2)}) collective-permute-start(bf16[4,160,384]{2,1,0:T(8,128)(2,1)S(1)} %collective-permute-done.8.rest_1_), channel_id=1, source_target_pairs={{0,2},{1,5},{2,0},{3,7},{4,6},{5,1},{6,4},{7,3},{8,10},{9,13},{10,... | collective-permute-start | bytes 1474568 | tf_op jit(solution)/shard_map/ppermute | solution.py:107
  35.8 14.4 %collective-permute-start.12 = (bf16[4,160,384]{2,1,0:T(8,128)(2,1)S(1)}, bf16[4,160,384]{2,1,0:T(8,128)(2,1)}, u32[]{:S(2)}, u32[]{:S(2)}) collective-permute-start(bf16[4,160,384]{2,1,0:T(8,128)(2,1)S(1)} %pad_maximum_fusion.1.rest_0_), channel_id=1, source_target_pairs={{0,1},{1,0},{2,3},{3,2},{4,5},{5,4},{6,7},{7,6},{8,9},{9,8},{10,11... | collective-permute-start | bytes 1474568 | tf_op jit(solution)/shard_map/ppermute | solution.py:107
  43.8 15.7 %collective-permute-start.10 = (bf16[4,272,384]{2,1,0:T(8,128)(2,1)S(1)}, bf16[4,272,384]{2,1,0:T(8,128)(2,1)}, u32[]{:S(2)}, u32[]{:S(2)}) collective-permute-start(bf16[4,272,384]{2,1,0:T(8,128)(2,1)S(1)} %pad_maximum_fusion.rest_0_), channel_id=1, source_target_pairs={{0,4},{1,3},{2,6},{3,1},{4,0},{5,7},{6,2},{7,5},{8,12},{9,11},{10,... | collective-permute-start | bytes 2506760 | tf_op jit(solution)/shard_map/ppermute | solution.py:107
  50.3 23.6 %collective-permute-start.19 = (bf16[4,272,384]{2,1,0:T(8,128)(2,1)S(1)}, bf16[4,272,384]{2,1,0:T(8,128)(2,1)}, u32[]{:S(2)}, u32[]{:S(2)}) collective-permute-start(bf16[4,272,384]{2,1,0:T(8,128)(2,1)S(1)} %pad_maximum_fusion.rest_0_), channel_id=1, source_target_pairs={{0,2},{1,5},{2,0},{3,7},{4,6},{5,1},{6,4},{7,3},{8,10},{9,13},{10,... | collective-permute-start | bytes 2506760 | tf_op jit(solution)/shard_map/ppermute | solution.py:107
  59.6 21.1 %collective-permute-start.16 = (bf16[4,272,384]{2,1,0:T(8,128)(2,1)}, bf16[4,272,384]{2,1,0:T(8,128)(2,1)}, u32[]{:S(2)}, u32[]{:S(2)}) collective-permute-start(bf16[4,272,384]{2,1,0:T(8,128)(2,1)} %collective-permute-done.10.rest_1_), channel_id=1, source_target_pairs={{0,2},{1,5},{2,0},{3,7},{4,6},{5,1},{6,4},{7,3},{8,10},{9,13},{10,... | collective-permute-start | bytes 2506760 | tf_op jit(solution)/shard_map/ppermute | solution.py:107
  61.4 9.3 %collective-permute-start.17 = (bf16[64,1536]{1,0:T(8,128)(2,1)S(1)}, bf16[64,1536]{1,0:T(8,128)(2,1)S(1)}, u32[]{:S(2)}, u32[]{:S(2)}) collective-permute-start(bf16[64,1536]{1,0:T(8,128)(2,1)S(1)} %get-tuple-element.91), channel_id=1, source_target_pairs={{0,1},{1,2},{2,3},{3,4},{4,5},{5,6},{6,7},{7,8},{8,9},{9,10},{10,1... | collective-permute-start | bytes 589832 | tf_op jit(solution)/shard_map/ppermute | solution.py:107
  65.8 11.6 %collective-permute-start.18 = (bf16[64,1536]{1,0:T(8,128)(2,1)S(1)}, bf16[64,1536]{1,0:T(8,128)(2,1)S(1)}, u32[]{:S(2)}, u32[]{:S(2)}) collective-permute-start(bf16[64,1536]{1,0:T(8,128)(2,1)S(1)} %get-tuple-element.90), channel_id=1, source_target_pairs={{1,0},{2,1},{3,2},{4,3},{5,4},{6,5},{7,6},{8,7},{9,8},{10,9},{11,1... | collective-permute-start | bytes 589832 | tf_op jit(solution)/shard_map/ppermute | solution.py:107
  68.0 12.8 %collective-permute-start.20 = (bf16[4,272,384]{2,1,0:T(8,128)(2,1)S(1)}, bf16[4,272,384]{2,1,0:T(8,128)(2,1)}, u32[]{:S(2)}, u32[]{:S(2)}) collective-permute-start(bf16[4,272,384]{2,1,0:T(8,128)(2,1)S(1)} %pad_maximum_fusion.rest_0_), channel_id=1, source_target_pairs={{0,1},{1,0},{2,3},{3,2},{4,5},{5,4},{6,7},{7,6},{8,9},{9,8},{10,11... | collective-permute-start | bytes 2506760 | tf_op jit(solution)/shard_map/ppermute | solution.py:107
  70.7 10.2 %collective-permute-start.21 = (bf16[4,272,384]{2,1,0:T(8,128)(2,1)}, bf16[4,272,384]{2,1,0:T(8,128)(2,1)}, u32[]{:S(2)}, u32[]{:S(2)}) collective-permute-start(bf16[4,272,384]{2,1,0:T(8,128)(2,1)} %collective-permute-done.10.rest_1_), channel_id=1, source_target_pairs={{0,1},{1,0},{2,3},{3,2},{4,5},{5,4},{6,7},{7,6},{8,9},{9,8},{10,11... | collective-permute-start | bytes 2506760 | tf_op jit(solution)/shard_map/ppermute | solution.py:107
  73.9 7.0 %collective-permute-start.22 = (bf16[4,272,384]{2,1,0:T(8,128)(2,1)}, bf16[4,272,384]{2,1,0:T(8,128)(2,1)}, u32[]{:S(2)}, u32[]{:S(2)}) collective-permute-start(bf16[4,272,384]{2,1,0:T(8,128)(2,1)} %collective-permute-done.19.rest_2_), channel_id=1, source_target_pairs={{0,1},{1,0},{2,3},{3,2},{4,5},{5,4},{6,7},{7,6},{8,9},{9,8},{10,11... | collective-permute-start | bytes 2506760 | tf_op jit(solution)/shard_map/ppermute | solution.py:107
  101.2 13.1 %collective-permute-start.24 = (bf16[16,272,384]{2,1,0:T(8,128)(2,1)}, bf16[16,272,384]{2,1,0:T(8,128)(2,1)S(1)}, u32[]{:S(2)}, u32[]{:S(2)}) collective-permute-start(bf16[16,272,384]{2,1,0:T(8,128)(2,1)} %get-tuple-element.61), channel_id=1, source_target_pairs={{0,1},{1,0},{2,3},{3,2},{4,5},{5,4},{6,7},{7,6},{8,9},{9,8},{10,11... | collective-permute-start | bytes 10027016 | tf_op jit(solution)/shard_map/ppermute | solution.py:107
  108.8 8.7 %collective-permute-start.25 = (bf16[64,1536]{1,0:T(8,128)(2,1)S(1)}, bf16[64,1536]{1,0:T(8,128)(2,1)S(1)}, u32[]{:S(2)}, u32[]{:S(2)}) collective-permute-start(bf16[64,1536]{1,0:T(8,128)(2,1)S(1)} %get-tuple-element.62), channel_id=1, source_target_pairs={{1,0},{2,1},{3,2},{4,3},{5,4},{6,5},{7,6},{8,7},{9,8},{10,9},{11,1... | collective-permute-start | bytes 589832 | tf_op jit(solution)/shard_map/ppermute | solution.py:107
  111.1 6.9 %collective-permute-start.26 = (bf16[64,1536]{1,0:T(8,128)(2,1)S(1)}, bf16[64,1536]{1,0:T(8,128)(2,1)S(1)}, u32[]{:S(2)}, u32[]{:S(2)}) collective-permute-start(bf16[64,1536]{1,0:T(8,128)(2,1)S(1)} %get-tuple-element.63), channel_id=1, source_target_pairs={{0,1},{1,2},{2,3},{3,4},{4,5},{5,6},{6,7},{7,8},{8,9},{9,10},{10,1... | collective-permute-start | bytes 589832 | tf_op jit(solution)/shard_map/ppermute | solution.py:107
  118.0 20.6 %collective-permute-start.27 = (bf16[8,272,384]{2,1,0:T(8,128)(2,1)S(1)}, bf16[8,272,384]{2,1,0:T(8,128)(2,1)S(1)}, u32[]{:S(2)}, u32[]{:S(2)}) collective-permute-start(bf16[8,272,384]{2,1,0:T(8,128)(2,1)S(1)} %slice.257), channel_id=1, source_target_pairs={{0,4},{1,3},{2,6},{3,1},{4,0},{5,7},{6,2},{7,5},{8,12},{9,11},{10,... | collective-permute-start | bytes 5013512 | tf_op jit(solution)/shard_map/ppermute | solution.py:107
  138.9 7.5 %collective-permute-start.28 = (bf16[16,160,384]{2,1,0:T(8,128)(2,1)S(1)}, bf16[16,160,384]{2,1,0:T(8,128)(2,1)S(1)}, u32[]{:S(2)}, u32[]{:S(2)}) collective-permute-start(bf16[16,160,384]{2,1,0:T(8,128)(2,1)S(1)} %copy-done.14), channel_id=1, source_target_pairs={{0,1},{1,0},{2,3},{3,2},{4,5},{5,4},{6,7},{7,6},{8,9},{9,8},{10,11... | collective-permute-start | bytes 5898248 | tf_op jit(solution)/shard_map/ppermute | solution.py:107
  143.0 15.6 %collective-permute-start.29 = (bf16[4,272,384]{2,1,0:T(8,128)(2,1)S(1)}, bf16[4,272,384]{2,1,0:T(8,128)(2,1)S(1)}, u32[]{:S(2)}, u32[]{:S(2)}) collective-permute-start(bf16[4,272,384]{2,1,0:T(8,128)(2,1)S(1)} %get-tuple-element.84), channel_id=1, source_target_pairs={{0,2},{1,5},{2,0},{3,7},{4,6},{5,1},{6,4},{7,3},{8,10},{9,13},{10,... | collective-permute-start | bytes 2506760 | tf_op jit(solution)/shard_map/ppermute | solution.py:107
  147.2 18.5 %collective-permute-start.31 = (bf16[8,160,384]{2,1,0:T(8,128)(2,1)S(1)}, bf16[8,160,384]{2,1,0:T(8,128)(2,1)S(1)}, u32[]{:S(2)}, u32[]{:S(2)}) collective-permute-start(bf16[8,160,384]{2,1,0:T(8,128)(2,1)S(1)} %get-tuple-element.82), channel_id=1, source_target_pairs={{0,4},{1,3},{2,6},{3,1},{4,0},{5,7},{6,2},{7,5},{8,12},{9,11},{10,... | collective-permute-start | bytes 2949128 | tf_op jit(solution)/shard_map/ppermute | solution.py:107
  166.0 8.0 %collective-permute-start.32 = (bf16[4,160,384]{2,1,0:T(8,128)(2,1)S(1)}, bf16[4,160,384]{2,1,0:T(8,128)(2,1)S(1)}, u32[]{:S(2)}, u32[]{:S(2)}) collective-permute-start(bf16[4,160,384]{2,1,0:T(8,128)(2,1)S(1)} %slice.264), channel_id=1, source_target_pairs={{0,2},{1,5},{2,0},{3,7},{4,6},{5,1},{6,4},{7,3},{8,10},{9,13},{10,... | collective-permute-start | bytes 1474568 | tf_op jit(solution)/shard_map/ppermute | solution.py:107
  166.2 15.7 %collective-permute-start.37 = (bf16[272,384]{1,0:T(8,128)(2,1)S(1)}, bf16[272,384]{1,0:T(8,128)(2,1)S(1)}, u32[]{:S(2)}, u32[]{:S(2)}) collective-permute-start(bf16[272,384]{1,0:T(8,128)(2,1)S(1)} %get-tuple-element.86), channel_id=1, source_target_pairs={{0,16},{1,17},{2,18},{3,19},{4,20},{5,21},{6,22},{7,23},{8,24},{9,... | collective-permute-start | bytes 626696 | tf_op jit(solution)/shard_map/ppermute | solution.py:107
  168.1 13.8 %collective-permute-start.38 = (bf16[272,384]{1,0:T(8,128)(2,1)S(1)}, bf16[272,384]{1,0:T(8,128)(2,1)S(1)}, u32[]{:S(2)}, u32[]{:S(2)}) collective-permute-start(bf16[272,384]{1,0:T(8,128)(2,1)S(1)} %get-tuple-element.87), channel_id=1, source_target_pairs={{0,24},{1,25},{2,26},{3,27},{4,28},{5,29},{6,30},{7,31},{8,0},{9,1... | collective-permute-start | bytes 626696 | tf_op jit(solution)/shard_map/ppermute | solution.py:107
  182.2 6.0 %collective-permute-start.33 = (bf16[160,384]{1,0:T(8,128)(2,1)S(1)}, bf16[160,384]{1,0:T(8,128)(2,1)S(1)}, u32[]{:S(2)}, u32[]{:S(2)}) collective-permute-start(bf16[160,384]{1,0:T(8,128)(2,1)S(1)} %get-tuple-element.92), channel_id=1, source_target_pairs={{0,8},{1,9},{2,10},{3,11},{4,12},{5,13},{6,14},{7,15},{8,16},{9,17... | collective-permute-start | bytes 368648 | tf_op jit(solution)/shard_map/ppermute | solution.py:107
  182.2 10.6 %collective-permute-start.34 = (bf16[160,384]{1,0:T(8,128)(2,1)S(1)}, bf16[160,384]{1,0:T(8,128)(2,1)S(1)}, u32[]{:S(2)}, u32[]{:S(2)}) collective-permute-start(bf16[160,384]{1,0:T(8,128)(2,1)S(1)} %get-tuple-element.94), channel_id=1, source_target_pairs={{0,16},{1,17},{2,18},{3,19},{4,20},{5,21},{6,22},{7,23},{8,24},{9,... | collective-permute-start | bytes 368648 | tf_op jit(solution)/shard_map/ppermute | solution.py:107
  185.4 11.6 %collective-permute-start.35 = (bf16[160,384]{1,0:T(8,128)(2,1)S(1)}, bf16[160,384]{1,0:T(8,128)(2,1)S(1)}, u32[]{:S(2)}, u32[]{:S(2)}) collective-permute-start(bf16[160,384]{1,0:T(8,128)(2,1)S(1)} %get-tuple-element.93), channel_id=1, source_target_pairs={{0,24},{1,25},{2,26},{3,27},{4,28},{5,29},{6,30},{7,31},{8,0},{9,1... | collective-permute-start | bytes 368648 | tf_op jit(solution)/shard_map/ppermute | solution.py:107
  186.8 11.4 %collective-permute-start.39 = (f32[128,384]{1,0:T(8,128)S(1)}, f32[128,384]{1,0:T(8,128)S(1)}, u32[]{:S(2)}, u32[]{:S(2)}) collective-permute-start(f32[128,384]{1,0:T(8,128)S(1)} %pad_maximum_fusion.2), channel_id=1, source_target_pairs={{0,1},{1,0},{2,3},{3,2},{4,5},{5,4},{6,7},{7,6},{8,9},{9,8},{10,11... | collective-permute-start | bytes 589832 | tf_op jit(solution)/shard_map/ppermute | solution.py:107
  (24 other events, 203.6 us)
where the time goes:
time: 202 us
  waiting for transfers between devices  81 us (40%)
  starting transfers between devices  47.6 us (24%)
  Pallas kernels  42.5 us (21%)
  other arithmetic  16.7 us (8%)
  local copies, waits for them, and re-layouts  10.5 us (5%)
  between operations  3.28 us (2%)
    ppermute x40, waiting for transfers between devices, permute(): return lax.ppermute(values, 'fsdp', pairs)  81 us
    ppermute x40, starting transfers between devices, permute(): return lax.ppermute(values, 'fsdp', pairs)  47.6 us
    pallas_call x5, Pallas kernels, call(): pl.pallas_call(kernel, out_shape=[jax.ShapeDtypeStruct(shape, kind) for s...  42.5 us
  transfers between devices with their start and end apart: 40, of which 19 were waited for; matrix products, arithmetic and copies ran while one was open for 10% of the time, Pallas kernels for 13%

commit v1 on v0

--- a/solution.py
+++ b/solution.py
@@ -1,3 +1,4 @@
+import functools
 import math
 
 import jax
@@ -320,16 +321,18 @@
     return lax.dot_general(left, right, (((0,), (0,)), ((), ())), preferred_element_type=jnp.float32)
 
 
-def call(kernel, outs, scratch, args, micros, blocks=0):
+def call(kernel, outs, scratch, args, micros, blocks=0, away=0):
     whole = len(args) - blocks - 1
     spaces = [pl.BlockSpec(memory_space=SMEM)] + [pl.BlockSpec(memory_space=VMEM)] * whole
     spaces += [pl.BlockSpec(memory_space=pl.ANY)] * blocks
     semaphores = [pltpu.SemaphoreType.DMA((2 * CHIPS, 4))] if blocks else []
+    semaphores += [pltpu.SemaphoreType.DMA((8,))] if away else []
+    near_outs = len(outs) - away
     return pl.pallas_call(
         kernel,
         out_shape=[jax.ShapeDtypeStruct(shape, kind) for shape, kind in outs],
         in_specs=spaces,
-        out_specs=[pl.BlockSpec(memory_space=VMEM)] * len(outs),
+        out_specs=[pl.BlockSpec(memory_space=VMEM)] * near_outs + [pl.BlockSpec(memory_space=pl.ANY)] * away,
         scratch_shapes=[pltpu.VMEM(shape, kind) for shape, kind in scratch] + semaphores,
         compiler_params=pltpu.CompilerParams(vmem_limit_bytes=LIMIT),
         cost_estimate=pl.CostEstimate(flops=0, bytes_accessed=3_690_000 * micros, transcendentals=0),
@@ -457,7 +460,13 @@
 
 def middle_kernel(place, tokens, mixed, gain, cotangent, *rest):
     refs = rest[:8]
-    block_out, d_after_out, d_mixed, send, keep, w_up, w_out, w_down, d_proj, hidden, done = rest[8:]
+    (block_out, d_after_out, d_mixed, send_out, keep_out, w_up, w_out, w_down, d_proj, hidden, send, keep, done, sent) = rest[8:]
+
+    def leave(start, count, kind):
+        rows = (slice(None), slice(start, start + count), slice(None))
+        pairs = ((send, send_out), (keep, keep_out))
+        return [pltpu.make_async_copy(a.at[rows], b.at[rows], sent.at[kind + i]) for i, (a, b) in enumerate(pairs)]
+
     out_copies = block_copies(place, refs, w_out, done, 0, 144, 48)
     up_copies = block_copies(place, refs, w_up, done, 1, 0, 144)
     down_copies = block_copies(place, refs, w_down, done, 2, 192, 48)
@@ -494,23 +503,31 @@
         d_proj[:, FF + HALF * j : FF + HALF * (j + 1)] = (d_hidden * active).astype(jnp.bfloat16)
     block_out[...] = jnp.where(live, after_attn + down, 0.0).astype(jnp.bfloat16)
     everyone = list(range(CHIPS))
+    for j in range(2):
+        up = tn_dot(d_proj[:, FF * j : FF * (j + 1)], a2)
+        put_both(place, send, keep, 0, up, everyone[8 * j : 8 * j + 8])
+    up_leave = leave(0, 144, 0)
+    go(up_leave)
+    down_grad = tn_dot(out_grad, hidden[...])
+    put_both(place, send, keep, 192, down_grad, everyone)
+    rest = down_grad[:, 2 * HALF :]
+    for chip in everyone:
+        put_rows(place, send, keep, 0, 240, rest[48 * chip : 48 * chip + 32], [chip])
+        put_rows(place, send, keep, 1, 240, rest[48 * chip + 32 : 48 * chip + 48], [chip])
+    down_leave = leave(192, 64, 2)
+    go(down_leave)
     d_second = nn_dot(d_proj[...], w_up[...])
     gain_grad = jnp.sum(normed * d_second, axis=0, keepdims=True)
     d_after = grad + norm_back(d_second * gains, normed, factor)
     d_after_out[...] = d_after
     d_attn = d_after.astype(jnp.bfloat16)
     d_mixed[...] = nn_dot(d_attn, w_out[...]).astype(jnp.bfloat16)
-    for j in range(2):
-        up = tn_dot(d_proj[:, FF * j : FF * (j + 1)], a2)
-        put_both(place, send, keep, 0, up, everyone[8 * j : 8 * j + 8])
     put_both(place, send, keep, 144, tn_dot(d_attn, mixed[...]), everyone)
-    down_grad = tn_dot(out_grad, hidden[...])
-    put_both(place, send, keep, 192, down_grad, everyone)
-    rest = down_grad[:, 2 * HALF :]
     for chip in everyone:
-        put_rows(place, send, keep, 0, 240, rest[48 * chip : 48 * chip + 32], [chip])
-        put_rows(place, send, keep, 1, 240, rest[48 * chip + 32 : 48 * chip + 48], [chip])
         put_rows(place, send, keep, 1, 256, gain_rows(gain_grad, chip), [chip])
+    out_leave, gain_leave = leave(144, 48, 4), leave(256, 16, 6)
+    go(out_leave + gain_leave)
+    land(up_leave + down_leave + out_leave + gain_leave)
 
 
 def attend_back_kernel(
@@ -720,10 +737,12 @@
     block_out, d_after, d_mixed, send, keep = call(
         middle_kernel,
         [((SLOTS, D), bf16), ((SLOTS, D), f32), ((SLOTS, D), bf16), ((CHIPS, ROWS2, HALF), bf16), ((CHIPS, ROWS2, HALF), bf16)],
-        [((2 * FF, D), bf16), ((D, D), bf16), ((D, FF), bf16), ((SLOTS, 2 * FF), bf16), ((SLOTS, FF), bf16)],
+        [((2 * FF, D), bf16), ((D, D), bf16), ((D, FF), bf16), ((SLOTS, 2 * FF), bf16), ((SLOTS, FF), bf16)]
+        + [((CHIPS, ROWS2, HALF), bf16)] * 2,
         [place, tokens, mixed, gain_m, cotangent] + blocks_two,
         14,
         8,
+        2,
     )
     d_query, d_own, rim_before, rim_after = call(
         attend_back_kernel,
@@ -785,7 +804,9 @@
     up_sum, out_sum = both[:72].T, both[72:96].T
     down_sum = jnp.concatenate([both[96:], last], axis=1).T
     gain_m_sum = jnp.where(core == 0, got[120, :24], gain_row[0, 24:48])
-    share = sum_shares(total_qkv[3], last_qkv)
+    done = (total_qkv[3], up_sum, out_sum, down_sum, gain_m_sum)
+    share, up_sum, out_sum, down_sum, gain_m_sum = lax.optimization_barrier(done)
+    share = sum_shares(share, last_qkv)
     got = permute(part(share, 0, 72, 1 - core), sibling)
     own = part(share, 0, 72, core)
     qkv_sum = jnp.concatenate([jnp.where(core == 0, own, got), jnp.where(core == 0, got, own)], axis=1).T

time: 202 us -> 200 us (0.990)
  transfers between devices with their start and end apart: 40 -> 40, of which waited for: 19 -> 20; matrix products, arithmetic and copies ran while one was open for 10% -> 10% of each run, Pallas kernels for 13% -> 13%
where the time goes in v1:
time: 200 us; the launch traced here: 199 us
  waiting for transfers between devices  80.2 us (40%)
  starting transfers between devices  46.7 us (23%)
  Pallas kernels  41.6 us (21%)
  other arithmetic  16.7 us (8%)
  local copies, waits for them, and re-layouts  10.6 us (5%)
  between operations  3.28 us (2%)
    ppermute x40, waiting for transfers between devices, permute(): return lax.ppermute(values, 'fsdp', pairs)  80.2 us
    ppermute x40, starting transfers between devices, permute(): return lax.ppermute(values, 'fsdp', pairs)  46.7 us
    pallas_call x5, Pallas kernels, call(): pl.pallas_call(kernel, out_shape=[jax.ShapeDtypeStruct(shape, kind) for s...  41.6 us
  transfers between devices with their start and end apart: 40, of which 20 were waited for; matrix products, arithmetic and copies ran while one was open for 10% of the time, Pallas kernels for 13%

profile of v1, /device:TPU:13, one launch (start us, length us, event | category | flops | bytes accessed | tf_op | source)
XLA Modules:
  0.0 199.0 jit_solution(16822450543109254918)
XLA Ops:
  11.7 7.0 %collective-permute-done.2 = bf16[160,384]{1,0:T(8,128)(2,1)S(1)} collective-permute-done((bf16[160,384]{1,0:T(8,128)(2,1)S(1)}, bf16[160,384]{1,0:T(8,128)(2,1)S(1)}, u32[]{:S(2)}, u32[]{:S(2)}) %collective-permute-start.2) | collective-permute-done | bytes 122912 | tf_op jit(solution)/shard_map/ppermute | solution.py:108
  18.7 2.5 %collective-permute-done.3 = bf16[160,384]{1,0:T(8,128)(2,1)S(1)} collective-permute-done((bf16[160,384]{1,0:T(8,128)(2,1)S(1)}, bf16[160,384]{1,0:T(8,128)(2,1)S(1)}, u32[]{:S(2)}, u32[]{:S(2)}) %collective-permute-start.3) | collective-permute-done | bytes 122912 | tf_op jit(solution)/shard_map/ppermute | solution.py:108
  27.4 5.9 %collective-permute-done.8.rest_1_ = bf16[4,160,384]{2,1,0:T(8,128)(2,1)S(1)} collective-permute-done((bf16[4,160,384]{2,1,0:T(8,128)(2,1)S(1)}, bf16[4,160,384]{2,1,0:T(8,128)(2,1)S(1)}, u32[]{:S(2)}, u32[]{:S(2)}) %collective-permute-start.8) | collective-permute-done | bytes 491552 | tf_op jit(solution)/shard_map/ppermute | solution.py:108
  35.8 3.6 %collective-permute-start.12 = (bf16[4,160,384]{2,1,0:T(8,128)(2,1)S(1)}, bf16[4,160,384]{2,1,0:T(8,128)(2,1)}, u32[]{:S(2)}, u32[]{:S(2)}) collective-permute-start(bf16[4,160,384]{2,1,0:T(8,128)(2,1)S(1)} %pad_maximum_fusion.1.rest_0_), channel_id=1, source_target_pairs={{0,1},{1,0},{2,3},{3,2},{4,5},{5,4},{6,7},{7,6},{8,9},{9,8},{10,11... | collective-permute-start | bytes 1474568 | tf_op jit(solution)/shard_map/ppermute | solution.py:108
  40.0 2.6 %collective-permute-done.7 = bf16[272,384]{1,0:T(8,128)(2,1)} collective-permute-done((bf16[272,384]{1,0:T(8,128)(2,1)S(1)}, bf16[272,384]{1,0:T(8,128)(2,1)}, u32[]{:S(2)}, u32[]{:S(2)}) %collective-permute-start.7) | collective-permute-done | bytes 208928 | tf_op jit(solution)/shard_map/ppermute | solution.py:108
  46.0 1.8 collective-permute-start.13
  52.7 6.8 %shard_map.161 = (bf16[256,768]{1,0:T(8,128)(2,1)S(1)}, bf16[256,1536]{1,0:T(8,128)(2,1)}, bf16[256,768]{1,0:T(8,128)(2,1)S(1)}, bf16[2304,768]{1,0:T(8,128)(2,1)}) custom-call(s32[66]{0:T(128)S(1)} %concatenate.67.place, bf16[256,768]{1,0:T(8,128)(2,1)S(1)} %copy-done.1, f32[1,768]{1,0:T(1,128)S(1)} %reshape.217.gain, ...), custom_call_target="tpu_custom_call" | custom-call | bytes 22140000 | tf_op jit(solution)/shard_map/pallas_call | solution.py:331
  61.4 4.4 %collective-permute-start.17 = (bf16[64,1536]{1,0:T(8,128)(2,1)S(1)}, bf16[64,1536]{1,0:T(8,128)(2,1)S(1)}, u32[]{:S(2)}, u32[]{:S(2)}) collective-permute-start(bf16[64,1536]{1,0:T(8,128)(2,1)S(1)} %get-tuple-element.101), channel_id=1, source_target_pairs={{0,1},{1,2},{2,3},{3,4},{4,5},{5,6},{6,7},{7,8},{8,9},{9,10},{10,1... | collective-permute-start | bytes 589832 | tf_op jit(solution)/shard_map/ppermute | solution.py:108
  65.8 1.9 collective-permute-start.18
  68.0 2.6 %collective-permute-start.20 = (bf16[4,272,384]{2,1,0:T(8,128)(2,1)S(1)}, bf16[4,272,384]{2,1,0:T(8,128)(2,1)}, u32[]{:S(2)}, u32[]{:S(2)}) collective-permute-start(bf16[4,272,384]{2,1,0:T(8,128)(2,1)S(1)} %pad_maximum_fusion.rest_0_), channel_id=1, source_target_pairs={{0,1},{1,0},{2,3},{3,2},{4,5},{5,4},{6,7},{7,6},{8,9},{9,8},{10,11... | collective-permute-start | bytes 2506760 | tf_op jit(solution)/shard_map/ppermute | solution.py:108
  70.7 3.2 %collective-permute-start.21 = (bf16[4,272,384]{2,1,0:T(8,128)(2,1)}, bf16[4,272,384]{2,1,0:T(8,128)(2,1)}, u32[]{:S(2)}, u32[]{:S(2)}) collective-permute-start(bf16[4,272,384]{2,1,0:T(8,128)(2,1)} %collective-permute-done.10.rest_1_), channel_id=1, source_target_pairs={{0,1},{1,0},{2,3},{3,2},{4,5},{5,4},{6,7},{7,6},{8,9},{9,8},{10,11... | collective-permute-start | bytes 2506760 | tf_op jit(solution)/shard_map/ppermute | solution.py:108
  73.9 3.5 %collective-permute-done.18.after = bf16[64,1536]{1,0:T(8,128)(2,1)S(1)} collective-permute-done((bf16[64,1536]{1,0:T(8,128)(2,1)S(1)}, bf16[64,1536]{1,0:T(8,128)(2,1)S(1)}, u32[]{:S(2)}, u32[]{:S(2)}) %collective-permute-start.18) | collective-permute-done | bytes 196640 | tf_op jit(solution)/shard_map/ppermute | solution.py:108
  77.4 2.6 %shard_map.162.mixed = bf16[256,768]{1,0:T(8,128)(2,1)S(1)} custom-call(s32[66]{0:T(128)S(1)} %concatenate.67.place, bf16[256,768]{1,0:T(8,128)(2,1)S(1)} %get-tuple-element.55.query, bf16[256,1536]{1,0:T(8,128)(2,1)S(1)} %copy-done, bf16[64,1536]{1,0:T(8,128)(2,1)S(1)} %collective-permute-done.17.before, ...), custom_call_target="tpu_custom_call" | custom-call | bytes 11070000 | tf_op jit(solution)/shard_map/pallas_call | solution.py:331
  80.9 2.6 %collective-permute-done.23.rest_7_ = bf16[4,272,384]{2,1,0:T(8,128)(2,1)} collective-permute-done((bf16[4,272,384]{2,1,0:T(8,128)(2,1)}, bf16[4,272,384]{2,1,0:T(8,128)(2,1)}, u32[]{:S(2)}, u32[]{:S(2)}) %collective-permute-start.23) | collective-permute-done | bytes 835616 | tf_op jit(solution)/shard_map/ppermute | solution.py:108
  84.4 15.9 %shard_map.163 = (bf16[256,768]{1,0:T(8,128)(2,1)}, f32[256,768]{1,0:T(8,128)S(1)}, bf16[256,768]{1,0:T(8,128)(2,1)S(1)}, bf16[16,272,384]{2,1,0:T(8,128)(2,1)}, bf16[16,272,384]{2,1,0:T(8,128)(2,1)}) custom-call(s32[66]{0:T(128)S(1)} %concatenate.67.place, bf16[256,768]{1,0:T(8,128)(2,1)S(1)} %copy-done.1, bf16[256,768]{1,0:T(8,128)(2,1)S(1)} %shard_map.162.mixed, ...), custom_call_target="tpu_custom_call" | custom-call | bytes 51660000 | tf_op jit(solution)/shard_map/pallas_call | solution.py:331
  100.4 7.4 %shard_map.164 = (f32[256,768]{1,0:T(8,128)S(1)}, f32[256,1536]{1,0:T(8,128)S(1)}, bf16[64,1536]{1,0:T(8,128)(2,1)S(1)}, bf16[64,1536]{1,0:T(8,128)(2,1)S(1)}) custom-call(s32[66]{0:T(128)S(1)} %concatenate.67.place, bf16[256,768]{1,0:T(8,128)(2,1)S(1)} %get-tuple-element.55.query, bf16[256,1536]{1,0:T(8,128)(2,1)S(1)} %copy-done, ...), custom_call_target="tpu_custom_call" | custom-call | bytes 29520000 | tf_op jit(solution)/shard_map/pallas_call | solution.py:331
  107.8 2.3 %collective-permute-start.25 = (bf16[64,1536]{1,0:T(8,128)(2,1)S(1)}, bf16[64,1536]{1,0:T(8,128)(2,1)S(1)}, u32[]{:S(2)}, u32[]{:S(2)}) collective-permute-start(bf16[64,1536]{1,0:T(8,128)(2,1)S(1)} %get-tuple-element.67), channel_id=1, source_target_pairs={{1,0},{2,1},{3,2},{4,3},{5,4},{6,5},{7,6},{8,7},{9,8},{10,9},{11,1... | collective-permute-start | bytes 589832 | tf_op jit(solution)/shard_map/ppermute | solution.py:108
  110.2 3.2 %collective-permute-start.26 = (bf16[64,1536]{1,0:T(8,128)(2,1)S(1)}, bf16[64,1536]{1,0:T(8,128)(2,1)S(1)}, u32[]{:S(2)}, u32[]{:S(2)}) collective-permute-start(bf16[64,1536]{1,0:T(8,128)(2,1)S(1)} %get-tuple-element.68), channel_id=1, source_target_pairs={{0,1},{1,2},{2,3},{3,4},{4,5},{5,6},{6,7},{7,8},{8,9},{9,10},{10,1... | collective-permute-start | bytes 589832 | tf_op jit(solution)/shard_map/ppermute | solution.py:108
  113.4 2.9 %add.311 = bf16[16,272,384]{2,1,0:T(8,128)(2,1)S(1)} add(bf16[16,272,384]{2,1,0:T(8,128)(2,1)} %get-tuple-element.65, bf16[16,272,384]{2,1,0:T(8,128)(2,1)S(1)} %collective-permute-done.24) | non-fusion elementwise | flops 1671168 | bytes 10027008 | tf_op jit(solution)/shard_map/add | solution.py:620
  118.2 8.9 %shard_map.165 = (f32[256,768]{1,0:T(8,128)}, bf16[16,160,384]{2,1,0:T(8,128)(2,1)}, bf16[16,160,384]{2,1,0:T(8,128)(2,1)}) custom-call(s32[66]{0:T(128)S(1)} %concatenate.67.place, bf16[256,768]{1,0:T(8,128)(2,1)S(1)} %copy-done.1, bf16[256,768]{1,0:T(8,128)(2,1)S(1)} %copy-done.10, f32[1,768]{1,0:T(1,128)S(1)} %reshape.217.gain, ...), custom_call_target="tpu_custom_call" | custom-call | bytes 33210000 | tf_op jit(solution)/shard_map/pallas_call | solution.py:331
  127.1 10.6 %collective-permute-done.27 = bf16[8,272,384]{2,1,0:T(8,128)(2,1)S(1)} collective-permute-done((bf16[8,272,384]{2,1,0:T(8,128)(2,1)S(1)}, bf16[8,272,384]{2,1,0:T(8,128)(2,1)S(1)}, u32[]{:S(2)}, u32[]{:S(2)}) %collective-permute-start.27) | collective-permute-done | bytes 1671200 | tf_op jit(solution)/shard_map/ppermute | solution.py:108
  137.9 3.9 %collective-permute-start.28 = (bf16[16,160,384]{2,1,0:T(8,128)(2,1)S(1)}, bf16[16,160,384]{2,1,0:T(8,128)(2,1)S(1)}, u32[]{:S(2)}, u32[]{:S(2)}) collective-permute-start(bf16[16,160,384]{2,1,0:T(8,128)(2,1)S(1)} %copy-done.14), channel_id=1, source_target_pairs={{0,1},{1,0},{2,3},{3,2},{4,5},{5,4},{6,7},{7,6},{8,9},{9,8},{10,11... | collective-permute-start | bytes 5898248 | tf_op jit(solution)/shard_map/ppermute | solution.py:108
  142.2 3.3 %collective-permute-done.28 = bf16[16,160,384]{2,1,0:T(8,128)(2,1)S(1)} collective-permute-done((bf16[16,160,384]{2,1,0:T(8,128)(2,1)S(1)}, bf16[16,160,384]{2,1,0:T(8,128)(2,1)S(1)}, u32[]{:S(2)}, u32[]{:S(2)}) %collective-permute-start.28) | collective-permute-done | bytes 1966112 | tf_op jit(solution)/shard_map/ppermute | solution.py:108
  146.3 11.3 %collective-permute-done.29 = bf16[4,272,384]{2,1,0:T(8,128)(2,1)S(1)} collective-permute-done((bf16[4,272,384]{2,1,0:T(8,128)(2,1)S(1)}, bf16[4,272,384]{2,1,0:T(8,128)(2,1)S(1)}, u32[]{:S(2)}, u32[]{:S(2)}) %collective-permute-start.29) | collective-permute-done | bytes 835616 | tf_op jit(solution)/shard_map/ppermute | solution.py:108
  158.0 4.9 %collective-permute-done.30 = bf16[272,384]{1,0:T(8,128)(2,1)S(1)} collective-permute-done((bf16[272,384]{1,0:T(8,128)(2,1)S(1)}, bf16[272,384]{1,0:T(8,128)(2,1)S(1)}, u32[]{:S(2)}, u32[]{:S(2)}) %collective-permute-start.30) | collective-permute-done | bytes 208928 | tf_op jit(solution)/shard_map/ppermute | solution.py:108
  162.9 1.9 collective-permute-done.31
  165.3 1.9 collective-permute-start.33
  167.4 5.8 %collective-permute-done.32 = bf16[4,160,384]{2,1,0:T(8,128)(2,1)S(1)} collective-permute-done((bf16[4,160,384]{2,1,0:T(8,128)(2,1)S(1)}, bf16[4,160,384]{2,1,0:T(8,128)(2,1)S(1)}, u32[]{:S(2)}, u32[]{:S(2)}) %collective-permute-start.32) | collective-permute-done | bytes 491552 | tf_op jit(solution)/shard_map/ppermute | solution.py:108
  173.2 7.8 %collective-permute-done.33 = bf16[272,384]{1,0:T(8,128)(2,1)S(1)} collective-permute-done((bf16[272,384]{1,0:T(8,128)(2,1)S(1)}, bf16[272,384]{1,0:T(8,128)(2,1)S(1)}, u32[]{:S(2)}, u32[]{:S(2)}) %collective-permute-start.33) | collective-permute-done | bytes 208928 | tf_op jit(solution)/shard_map/ppermute | solution.py:108
  181.9 3.1 %collective-permute-start.37 = (bf16[160,384]{1,0:T(8,128)(2,1)S(1)}, bf16[160,384]{1,0:T(8,128)(2,1)S(1)}, u32[]{:S(2)}, u32[]{:S(2)}) collective-permute-start(bf16[160,384]{1,0:T(8,128)(2,1)S(1)} %get-tuple-element.104), channel_id=1, source_target_pairs={{0,16},{1,17},{2,18},{3,19},{4,20},{5,21},{6,22},{7,23},{8,24},{9,... | collective-permute-start | bytes 368648 | tf_op jit(solution)/shard_map/ppermute | solution.py:108
  189.1 4.0 %collective-permute-done.37 = bf16[160,384]{1,0:T(8,128)(2,1)S(1)} collective-permute-done((bf16[160,384]{1,0:T(8,128)(2,1)S(1)}, bf16[160,384]{1,0:T(8,128)(2,1)S(1)}, u32[]{:S(2)}, u32[]{:S(2)}) %collective-permute-start.37) | collective-permute-done | bytes 122912 | tf_op jit(solution)/shard_map/ppermute | solution.py:108
  193.0 3.7 %collective-permute-done.38 = bf16[160,384]{1,0:T(8,128)(2,1)S(1)} collective-permute-done((bf16[160,384]{1,0:T(8,128)(2,1)S(1)}, bf16[160,384]{1,0:T(8,128)(2,1)S(1)}, u32[]{:S(2)}, u32[]{:S(2)}) %collective-permute-start.38) | collective-permute-done | bytes 122912 | tf_op jit(solution)/shard_map/ppermute | solution.py:108
  (173 shorter events, 41.9 us)
Async XLA Ops:
  5.5 5.6 %collective-permute-start.4 = (bf16[128,384]{1,0:T(8,128)(2,1)S(1)}, bf16[128,384]{1,0:T(8,128)(2,1)S(1)}, u32[]{:S(2)}, u32[]{:S(2)}) collective-permute-start(bf16[128,384]{1,0:T(8,128)(2,1)S(1)} %pad_maximum_fusion.10), channel_id=1, source_target_pairs={{0,1},{1,0},{2,3},{3,2},{4,5},{5,4},{6,7},{7,6},{8,9},{9,8},{10,11... | collective-permute-start | bytes 294920 | tf_op jit(solution)/shard_map/ppermute | solution.py:108
  8.6 10.2 %collective-permute-start.2 = (bf16[160,384]{1,0:T(8,128)(2,1)S(1)}, bf16[160,384]{1,0:T(8,128)(2,1)S(1)}, u32[]{:S(2)}, u32[]{:S(2)}) collective-permute-start(bf16[160,384]{1,0:T(8,128)(2,1)S(1)} %get-tuple-element.124), channel_id=1, source_target_pairs={{0,16},{1,17},{2,18},{3,19},{4,20},{5,21},{6,22},{7,23},{8,24},{9,... | collective-permute-start | bytes 368648 | tf_op jit(solution)/shard_map/ppermute | solution.py:108
  9.7 11.6 %collective-permute-start.3 = (bf16[160,384]{1,0:T(8,128)(2,1)S(1)}, bf16[160,384]{1,0:T(8,128)(2,1)S(1)}, u32[]{:S(2)}, u32[]{:S(2)}) collective-permute-start(bf16[160,384]{1,0:T(8,128)(2,1)S(1)} %get-tuple-element.124), channel_id=1, source_target_pairs={{0,24},{1,25},{2,26},{3,27},{4,28},{5,29},{6,30},{7,31},{8,0},{9,1... | collective-permute-start | bytes 368648 | tf_op jit(solution)/shard_map/ppermute | solution.py:108
  21.4 11.9 %collective-permute-start.8 = (bf16[4,160,384]{2,1,0:T(8,128)(2,1)S(1)}, bf16[4,160,384]{2,1,0:T(8,128)(2,1)S(1)}, u32[]{:S(2)}, u32[]{:S(2)}) collective-permute-start(bf16[4,160,384]{2,1,0:T(8,128)(2,1)S(1)} %pad_maximum_fusion.1.rest_0_), channel_id=1, source_target_pairs={{0,4},{1,3},{2,6},{3,1},{4,0},{5,7},{6,2},{7,5},{8,12},{9,11},{10,... | collective-permute-start | bytes 1474568 | tf_op jit(solution)/shard_map/ppermute | solution.py:108
  22.6 25.2 %collective-permute-start.11 = (bf16[4,160,384]{2,1,0:T(8,128)(2,1)S(1)}, bf16[4,160,384]{2,1,0:T(8,128)(2,1)S(1)}, u32[]{:S(2)}, u32[]{:S(2)}) collective-permute-start(bf16[4,160,384]{2,1,0:T(8,128)(2,1)S(1)} %pad_maximum_fusion.1.rest_0_), channel_id=1, source_target_pairs={{0,2},{1,5},{2,0},{3,7},{4,6},{5,1},{6,4},{7,3},{8,10},{9,13},{10,... | collective-permute-start | bytes 1474568 | tf_op jit(solution)/shard_map/ppermute | solution.py:108
  22.9 12.9 %collective-permute-start.5 = (bf16[272,384]{1,0:T(8,128)(2,1)S(1)}, bf16[272,384]{1,0:T(8,128)(2,1)S(1)}, u32[]{:S(2)}, u32[]{:S(2)}) collective-permute-start(bf16[272,384]{1,0:T(8,128)(2,1)S(1)} %fusion.14), channel_id=1, source_target_pairs={{0,8},{1,9},{2,10},{3,11},{4,12},{5,13},{6,14},{7,15},{8,16},{9,17... | collective-permute-start | bytes 626696 | tf_op jit(solution)/shard_map/ppermute | solution.py:108
  22.9 17.1 %collective-permute-start.6 = (bf16[272,384]{1,0:T(8,128)(2,1)S(1)}, bf16[272,384]{1,0:T(8,128)(2,1)}, u32[]{:S(2)}, u32[]{:S(2)}) collective-permute-start(bf16[272,384]{1,0:T(8,128)(2,1)S(1)} %fusion.14), channel_id=1, source_target_pairs={{0,16},{1,17},{2,18},{3,19},{4,20},{5,21},{6,22},{7,23},{8,24},{9,... | collective-permute-start | bytes 626696 | tf_op jit(solution)/shard_map/ppermute | solution.py:108
  23.5 19.2 %collective-permute-start.7 = (bf16[272,384]{1,0:T(8,128)(2,1)S(1)}, bf16[272,384]{1,0:T(8,128)(2,1)}, u32[]{:S(2)}, u32[]{:S(2)}) collective-permute-start(bf16[272,384]{1,0:T(8,128)(2,1)S(1)} %fusion.14), channel_id=1, source_target_pairs={{0,24},{1,25},{2,26},{3,27},{4,28},{5,29},{6,30},{7,31},{8,0},{9,1... | collective-permute-start | bytes 626696 | tf_op jit(solution)/shard_map/ppermute | solution.py:108
  33.2 10.6 %collective-permute-start.9 = (bf16[4,160,384]{2,1,0:T(8,128)(2,1)S(1)}, bf16[4,160,384]{2,1,0:T(8,128)(2,1)}, u32[]{:S(2)}, u32[]{:S(2)}) collective-permute-start(bf16[4,160,384]{2,1,0:T(8,128)(2,1)S(1)} %collective-permute-done.8.rest_1_), channel_id=1, source_target_pairs={{0,2},{1,5},{2,0},{3,7},{4,6},{5,1},{6,4},{7,3},{8,10},{9,13},{10,... | collective-permute-start | bytes 1474568 | tf_op jit(solution)/shard_map/ppermute | solution.py:108
  35.8 14.4 %collective-permute-start.12 = (bf16[4,160,384]{2,1,0:T(8,128)(2,1)S(1)}, bf16[4,160,384]{2,1,0:T(8,128)(2,1)}, u32[]{:S(2)}, u32[]{:S(2)}) collective-permute-start(bf16[4,160,384]{2,1,0:T(8,128)(2,1)S(1)} %pad_maximum_fusion.1.rest_0_), channel_id=1, source_target_pairs={{0,1},{1,0},{2,3},{3,2},{4,5},{5,4},{6,7},{7,6},{8,9},{9,8},{10,11... | collective-permute-start | bytes 1474568 | tf_op jit(solution)/shard_map/ppermute | solution.py:108
  43.8 15.7 %collective-permute-start.10 = (bf16[4,272,384]{2,1,0:T(8,128)(2,1)S(1)}, bf16[4,272,384]{2,1,0:T(8,128)(2,1)}, u32[]{:S(2)}, u32[]{:S(2)}) collective-permute-start(bf16[4,272,384]{2,1,0:T(8,128)(2,1)S(1)} %pad_maximum_fusion.rest_0_), channel_id=1, source_target_pairs={{0,4},{1,3},{2,6},{3,1},{4,0},{5,7},{6,2},{7,5},{8,12},{9,11},{10,... | collective-permute-start | bytes 2506760 | tf_op jit(solution)/shard_map/ppermute | solution.py:108
  50.3 23.6 %collective-permute-start.19 = (bf16[4,272,384]{2,1,0:T(8,128)(2,1)S(1)}, bf16[4,272,384]{2,1,0:T(8,128)(2,1)}, u32[]{:S(2)}, u32[]{:S(2)}) collective-permute-start(bf16[4,272,384]{2,1,0:T(8,128)(2,1)S(1)} %pad_maximum_fusion.rest_0_), channel_id=1, source_target_pairs={{0,2},{1,5},{2,0},{3,7},{4,6},{5,1},{6,4},{7,3},{8,10},{9,13},{10,... | collective-permute-start | bytes 2506760 | tf_op jit(solution)/shard_map/ppermute | solution.py:108
  59.6 21.1 %collective-permute-start.16 = (bf16[4,272,384]{2,1,0:T(8,128)(2,1)}, bf16[4,272,384]{2,1,0:T(8,128)(2,1)}, u32[]{:S(2)}, u32[]{:S(2)}) collective-permute-start(bf16[4,272,384]{2,1,0:T(8,128)(2,1)} %collective-permute-done.10.rest_1_), channel_id=1, source_target_pairs={{0,2},{1,5},{2,0},{3,7},{4,6},{5,1},{6,4},{7,3},{8,10},{9,13},{10,... | collective-permute-start | bytes 2506760 | tf_op jit(solution)/shard_map/ppermute | solution.py:108
  61.4 9.3 %collective-permute-start.17 = (bf16[64,1536]{1,0:T(8,128)(2,1)S(1)}, bf16[64,1536]{1,0:T(8,128)(2,1)S(1)}, u32[]{:S(2)}, u32[]{:S(2)}) collective-permute-start(bf16[64,1536]{1,0:T(8,128)(2,1)S(1)} %get-tuple-element.101), channel_id=1, source_target_pairs={{0,1},{1,2},{2,3},{3,4},{4,5},{5,6},{6,7},{7,8},{8,9},{9,10},{10,1... | collective-permute-start | bytes 589832 | tf_op jit(solution)/shard_map/ppermute | solution.py:108
  65.8 11.6 %collective-permute-start.18 = (bf16[64,1536]{1,0:T(8,128)(2,1)S(1)}, bf16[64,1536]{1,0:T(8,128)(2,1)S(1)}, u32[]{:S(2)}, u32[]{:S(2)}) collective-permute-start(bf16[64,1536]{1,0:T(8,128)(2,1)S(1)} %get-tuple-element.100), channel_id=1, source_target_pairs={{1,0},{2,1},{3,2},{4,3},{5,4},{6,5},{7,6},{8,7},{9,8},{10,9},{11,1... | collective-permute-start | bytes 589832 | tf_op jit(solution)/shard_map/ppermute | solution.py:108
  68.0 12.8 %collective-permute-start.20 = (bf16[4,272,384]{2,1,0:T(8,128)(2,1)S(1)}, bf16[4,272,384]{2,1,0:T(8,128)(2,1)}, u32[]{:S(2)}, u32[]{:S(2)}) collective-permute-start(bf16[4,272,384]{2,1,0:T(8,128)(2,1)S(1)} %pad_maximum_fusion.rest_0_), channel_id=1, source_target_pairs={{0,1},{1,0},{2,3},{3,2},{4,5},{5,4},{6,7},{7,6},{8,9},{9,8},{10,11... | collective-permute-start | bytes 2506760 | tf_op jit(solution)/shard_map/ppermute | solution.py:108
  70.7 10.2 %collective-permute-start.21 = (bf16[4,272,384]{2,1,0:T(8,128)(2,1)}, bf16[4,272,384]{2,1,0:T(8,128)(2,1)}, u32[]{:S(2)}, u32[]{:S(2)}) collective-permute-start(bf16[4,272,384]{2,1,0:T(8,128)(2,1)} %collective-permute-done.10.rest_1_), channel_id=1, source_target_pairs={{0,1},{1,0},{2,3},{3,2},{4,5},{5,4},{6,7},{7,6},{8,9},{9,8},{10,11... | collective-permute-start | bytes 2506760 | tf_op jit(solution)/shard_map/ppermute | solution.py:108
  73.9 7.0 %collective-permute-start.22 = (bf16[4,272,384]{2,1,0:T(8,128)(2,1)}, bf16[4,272,384]{2,1,0:T(8,128)(2,1)}, u32[]{:S(2)}, u32[]{:S(2)}) collective-permute-start(bf16[4,272,384]{2,1,0:T(8,128)(2,1)} %collective-permute-done.19.rest_2_), channel_id=1, source_target_pairs={{0,1},{1,0},{2,3},{3,2},{4,5},{5,4},{6,7},{7,6},{8,9},{9,8},{10,11... | collective-permute-start | bytes 2506760 | tf_op jit(solution)/shard_map/ppermute | solution.py:108
  100.3 13.1 %collective-permute-start.24 = (bf16[16,272,384]{2,1,0:T(8,128)(2,1)}, bf16[16,272,384]{2,1,0:T(8,128)(2,1)S(1)}, u32[]{:S(2)}, u32[]{:S(2)}) collective-permute-start(bf16[16,272,384]{2,1,0:T(8,128)(2,1)} %get-tuple-element.66), channel_id=1, source_target_pairs={{0,1},{1,0},{2,3},{3,2},{4,5},{5,4},{6,7},{7,6},{8,9},{9,8},{10,11... | collective-permute-start | bytes 10027016 | tf_op jit(solution)/shard_map/ppermute | solution.py:108
  107.8 8.7 %collective-permute-start.25 = (bf16[64,1536]{1,0:T(8,128)(2,1)S(1)}, bf16[64,1536]{1,0:T(8,128)(2,1)S(1)}, u32[]{:S(2)}, u32[]{:S(2)}) collective-permute-start(bf16[64,1536]{1,0:T(8,128)(2,1)S(1)} %get-tuple-element.67), channel_id=1, source_target_pairs={{1,0},{2,1},{3,2},{4,3},{5,4},{6,5},{7,6},{8,7},{9,8},{10,9},{11,1... | collective-permute-start | bytes 589832 | tf_op jit(solution)/shard_map/ppermute | solution.py:108
  110.2 6.9 %collective-permute-start.26 = (bf16[64,1536]{1,0:T(8,128)(2,1)S(1)}, bf16[64,1536]{1,0:T(8,128)(2,1)S(1)}, u32[]{:S(2)}, u32[]{:S(2)}) collective-permute-start(bf16[64,1536]{1,0:T(8,128)(2,1)S(1)} %get-tuple-element.68), channel_id=1, source_target_pairs={{0,1},{1,2},{2,3},{3,4},{4,5},{5,6},{6,7},{7,8},{8,9},{9,10},{10,1... | collective-permute-start | bytes 589832 | tf_op jit(solution)/shard_map/ppermute | solution.py:108
  117.1 20.6 %collective-permute-start.27 = (bf16[8,272,384]{2,1,0:T(8,128)(2,1)S(1)}, bf16[8,272,384]{2,1,0:T(8,128)(2,1)S(1)}, u32[]{:S(2)}, u32[]{:S(2)}) collective-permute-start(bf16[8,272,384]{2,1,0:T(8,128)(2,1)S(1)} %slice.257), channel_id=1, source_target_pairs={{0,4},{1,3},{2,6},{3,1},{4,0},{5,7},{6,2},{7,5},{8,12},{9,11},{10,... | collective-permute-start | bytes 5013512 | tf_op jit(solution)/shard_map/ppermute | solution.py:108
  137.9 7.5 %collective-permute-start.28 = (bf16[16,160,384]{2,1,0:T(8,128)(2,1)S(1)}, bf16[16,160,384]{2,1,0:T(8,128)(2,1)S(1)}, u32[]{:S(2)}, u32[]{:S(2)}) collective-permute-start(bf16[16,160,384]{2,1,0:T(8,128)(2,1)S(1)} %copy-done.14), channel_id=1, source_target_pairs={{0,1},{1,0},{2,3},{3,2},{4,5},{5,4},{6,7},{7,6},{8,9},{9,8},{10,11... | collective-permute-start | bytes 5898248 | tf_op jit(solution)/shard_map/ppermute | solution.py:108
  142.0 15.6 %collective-permute-start.29 = (bf16[4,272,384]{2,1,0:T(8,128)(2,1)S(1)}, bf16[4,272,384]{2,1,0:T(8,128)(2,1)S(1)}, u32[]{:S(2)}, u32[]{:S(2)}) collective-permute-start(bf16[4,272,384]{2,1,0:T(8,128)(2,1)S(1)} %get-tuple-element.94), channel_id=1, source_target_pairs={{0,2},{1,5},{2,0},{3,7},{4,6},{5,1},{6,4},{7,3},{8,10},{9,13},{10,... | collective-permute-start | bytes 2506760 | tf_op jit(solution)/shard_map/ppermute | solution.py:108
  146.3 18.5 %collective-permute-start.31 = (bf16[8,160,384]{2,1,0:T(8,128)(2,1)S(1)}, bf16[8,160,384]{2,1,0:T(8,128)(2,1)S(1)}, u32[]{:S(2)}, u32[]{:S(2)}) collective-permute-start(bf16[8,160,384]{2,1,0:T(8,128)(2,1)S(1)} %get-tuple-element.92), channel_id=1, source_target_pairs={{0,4},{1,3},{2,6},{3,1},{4,0},{5,7},{6,2},{7,5},{8,12},{9,11},{10,... | collective-permute-start | bytes 2949128 | tf_op jit(solution)/shard_map/ppermute | solution.py:108
  165.1 8.0 %collective-permute-start.32 = (bf16[4,160,384]{2,1,0:T(8,128)(2,1)S(1)}, bf16[4,160,384]{2,1,0:T(8,128)(2,1)S(1)}, u32[]{:S(2)}, u32[]{:S(2)}) collective-permute-start(bf16[4,160,384]{2,1,0:T(8,128)(2,1)S(1)} %slice.264), channel_id=1, source_target_pairs={{0,2},{1,5},{2,0},{3,7},{4,6},{5,1},{6,4},{7,3},{8,10},{9,13},{10,... | collective-permute-start | bytes 1474568 | tf_op jit(solution)/shard_map/ppermute | solution.py:108
  165.3 15.7 %collective-permute-start.33 = (bf16[272,384]{1,0:T(8,128)(2,1)S(1)}, bf16[272,384]{1,0:T(8,128)(2,1)S(1)}, u32[]{:S(2)}, u32[]{:S(2)}) collective-permute-start(bf16[272,384]{1,0:T(8,128)(2,1)S(1)} %get-tuple-element.96), channel_id=1, source_target_pairs={{0,16},{1,17},{2,18},{3,19},{4,20},{5,21},{6,22},{7,23},{8,24},{9,... | collective-permute-start | bytes 626696 | tf_op jit(solution)/shard_map/ppermute | solution.py:108
  167.2 13.8 %collective-permute-start.34 = (bf16[272,384]{1,0:T(8,128)(2,1)S(1)}, bf16[272,384]{1,0:T(8,128)(2,1)S(1)}, u32[]{:S(2)}, u32[]{:S(2)}) collective-permute-start(bf16[272,384]{1,0:T(8,128)(2,1)S(1)} %get-tuple-element.97), channel_id=1, source_target_pairs={{0,24},{1,25},{2,26},{3,27},{4,28},{5,29},{6,30},{7,31},{8,0},{9,1... | collective-permute-start | bytes 626696 | tf_op jit(solution)/shard_map/ppermute | solution.py:108
  181.3 5.2 %collective-permute-start.35 = (f32[128,384]{1,0:T(8,128)S(1)}, f32[128,384]{1,0:T(8,128)S(1)}, u32[]{:S(2)}, u32[]{:S(2)}) collective-permute-start(f32[128,384]{1,0:T(8,128)S(1)} %pad_maximum_fusion.2), channel_id=1, source_target_pairs={{0,1},{1,0},{2,3},{3,2},{4,5},{5,4},{6,7},{7,6},{8,9},{9,8},{10,11... | collective-permute-start | bytes 589832 | tf_op jit(solution)/shard_map/ppermute | solution.py:108
  181.9 7.2 %collective-permute-start.36 = (bf16[160,384]{1,0:T(8,128)(2,1)S(1)}, bf16[160,384]{1,0:T(8,128)(2,1)S(1)}, u32[]{:S(2)}, u32[]{:S(2)}) collective-permute-start(bf16[160,384]{1,0:T(8,128)(2,1)S(1)} %get-tuple-element.105), channel_id=1, source_target_pairs={{0,8},{1,9},{2,10},{3,11},{4,12},{5,13},{6,14},{7,15},{8,16},{9,17... | collective-permute-start | bytes 368648 | tf_op jit(solution)/shard_map/ppermute | solution.py:108
  181.9 11.1 %collective-permute-start.37 = (bf16[160,384]{1,0:T(8,128)(2,1)S(1)}, bf16[160,384]{1,0:T(8,128)(2,1)S(1)}, u32[]{:S(2)}, u32[]{:S(2)}) collective-permute-start(bf16[160,384]{1,0:T(8,128)(2,1)S(1)} %get-tuple-element.104), channel_id=1, source_target_pairs={{0,16},{1,17},{2,18},{3,19},{4,20},{5,21},{6,22},{7,23},{8,24},{9,... | collective-permute-start | bytes 368648 | tf_op jit(solution)/shard_map/ppermute | solution.py:108
  185.1 11.7 %collective-permute-start.38 = (bf16[160,384]{1,0:T(8,128)(2,1)S(1)}, bf16[160,384]{1,0:T(8,128)(2,1)S(1)}, u32[]{:S(2)}, u32[]{:S(2)}) collective-permute-start(bf16[160,384]{1,0:T(8,128)(2,1)S(1)} %get-tuple-element.103), channel_id=1, source_target_pairs={{0,24},{1,25},{2,26},{3,27},{4,28},{5,29},{6,30},{7,31},{8,0},{9,1... | collective-permute-start | bytes 368648 | tf_op jit(solution)/shard_map/ppermute | solution.py:108
  (24 other events, 199.5 us)

commit v2 on v1

--- a/solution.py
+++ b/solution.py
@@ -407,12 +407,11 @@
     c, sa, sb = cos[...], sin_a[...], sin_b[...]
     land(copies)
     for part in range(3):
-        for j in range(2):
-            base = part * D + HALF * j
-            joined = nt_dot(a1, weight[base : base + HALF, :])
-            for p in range(3):
-                lanes = slice(HALF * j + PAIR * p, HALF * j + PAIR * (p + 1))
-                v = joined[:, PAIR * p : PAIR * (p + 1)]
+        for j in range(1):
+            joined = nt_dot(a1, weight[part * D : (part + 1) * D, :])
+            for p in range(PAIRS):
+                lanes = slice(PAIR * p, PAIR * (p + 1))
+                v = joined[:, lanes]
                 if part < 2:
                     v = v * c + pltpu.roll(v, 96, 1) * sa + pltpu.roll(v, 32, 1) * sb
                 if part == 0:

time: 200 us -> 200 us (level)
  no operation moved by 1% of the time
where the time goes in v2:
time: 200 us; the launch traced here: 199 us
  waiting for transfers between devices  80.2 us (40%)
  starting transfers between devices  46.7 us (23%)
  Pallas kernels  41.6 us (21%)
  other arithmetic  16.7 us (8%)
  local copies, waits for them, and re-layouts  10.6 us (5%)
  between operations  3.28 us (2%)
    ppermute x40, waiting for transfers between devices, permute(): return lax.ppermute(values, 'fsdp', pairs)  80.2 us
    ppermute x40, starting transfers between devices, permute(): return lax.ppermute(values, 'fsdp', pairs)  46.7 us
    pallas_call x5, Pallas kernels, call(): pl.pallas_call(kernel, out_shape=[jax.ShapeDtypeStruct(shape, kind) for s...  41.6 us
  transfers between devices with their start and end apart: 40, of which 20 were waited for; matrix products, arithmetic and copies ran while one was open for 10% of the time, Pallas kernels for 13%

profile of v2, /device:TPU:13, one launch (start us, length us, event | category | flops | bytes accessed | tf_op | source)
XLA Modules:
  0.0 199.0 jit_solution(15652423460963451411)
XLA Ops:
  11.7 7.0 %collective-permute-done.2 = bf16[160,384]{1,0:T(8,128)(2,1)S(1)} collective-permute-done((bf16[160,384]{1,0:T(8,128)(2,1)S(1)}, bf16[160,384]{1,0:T(8,128)(2,1)S(1)}, u32[]{:S(2)}, u32[]{:S(2)}) %collective-permute-start.2) | collective-permute-done | bytes 122912 | tf_op jit(solution)/shard_map/ppermute | solution.py:108
  18.7 2.5 %collective-permute-done.3 = bf16[160,384]{1,0:T(8,128)(2,1)S(1)} collective-permute-done((bf16[160,384]{1,0:T(8,128)(2,1)S(1)}, bf16[160,384]{1,0:T(8,128)(2,1)S(1)}, u32[]{:S(2)}, u32[]{:S(2)}) %collective-permute-start.3) | collective-permute-done | bytes 122912 | tf_op jit(solution)/shard_map/ppermute | solution.py:108
  27.4 5.9 %collective-permute-done.8.rest_1_ = bf16[4,160,384]{2,1,0:T(8,128)(2,1)S(1)} collective-permute-done((bf16[4,160,384]{2,1,0:T(8,128)(2,1)S(1)}, bf16[4,160,384]{2,1,0:T(8,128)(2,1)S(1)}, u32[]{:S(2)}, u32[]{:S(2)}) %collective-permute-start.8) | collective-permute-done | bytes 491552 | tf_op jit(solution)/shard_map/ppermute | solution.py:108
  35.8 3.6 %collective-permute-start.12 = (bf16[4,160,384]{2,1,0:T(8,128)(2,1)S(1)}, bf16[4,160,384]{2,1,0:T(8,128)(2,1)}, u32[]{:S(2)}, u32[]{:S(2)}) collective-permute-start(bf16[4,160,384]{2,1,0:T(8,128)(2,1)S(1)} %pad_maximum_fusion.1.rest_0_), channel_id=1, source_target_pairs={{0,1},{1,0},{2,3},{3,2},{4,5},{5,4},{6,7},{7,6},{8,9},{9,8},{10,11... | collective-permute-start | bytes 1474568 | tf_op jit(solution)/shard_map/ppermute | solution.py:108
  40.0 2.6 %collective-permute-done.7 = bf16[272,384]{1,0:T(8,128)(2,1)} collective-permute-done((bf16[272,384]{1,0:T(8,128)(2,1)S(1)}, bf16[272,384]{1,0:T(8,128)(2,1)}, u32[]{:S(2)}, u32[]{:S(2)}) %collective-permute-start.7) | collective-permute-done | bytes 208928 | tf_op jit(solution)/shard_map/ppermute | solution.py:108
  46.0 1.8 collective-permute-start.13
  52.7 6.8 %shard_map.161 = (bf16[256,768]{1,0:T(8,128)(2,1)S(1)}, bf16[256,1536]{1,0:T(8,128)(2,1)}, bf16[256,768]{1,0:T(8,128)(2,1)S(1)}, bf16[2304,768]{1,0:T(8,128)(2,1)}) custom-call(s32[66]{0:T(128)S(1)} %concatenate.67.place, bf16[256,768]{1,0:T(8,128)(2,1)S(1)} %copy-done.1, f32[1,768]{1,0:T(1,128)S(1)} %reshape.217.gain, ...), custom_call_target="tpu_custom_call" | custom-call | bytes 22140000 | tf_op jit(solution)/shard_map/pallas_call | solution.py:331
  61.4 4.4 %collective-permute-start.17 = (bf16[64,1536]{1,0:T(8,128)(2,1)S(1)}, bf16[64,1536]{1,0:T(8,128)(2,1)S(1)}, u32[]{:S(2)}, u32[]{:S(2)}) collective-permute-start(bf16[64,1536]{1,0:T(8,128)(2,1)S(1)} %get-tuple-element.101), channel_id=1, source_target_pairs={{0,1},{1,2},{2,3},{3,4},{4,5},{5,6},{6,7},{7,8},{8,9},{9,10},{10,1... | collective-permute-start | bytes 589832 | tf_op jit(solution)/shard_map/ppermute | solution.py:108
  65.8 1.9 collective-permute-start.18
  68.0 2.6 %collective-permute-start.20 = (bf16[4,272,384]{2,1,0:T(8,128)(2,1)S(1)}, bf16[4,272,384]{2,1,0:T(8,128)(2,1)}, u32[]{:S(2)}, u32[]{:S(2)}) collective-permute-start(bf16[4,272,384]{2,1,0:T(8,128)(2,1)S(1)} %pad_maximum_fusion.rest_0_), channel_id=1, source_target_pairs={{0,1},{1,0},{2,3},{3,2},{4,5},{5,4},{6,7},{7,6},{8,9},{9,8},{10,11... | collective-permute-start | bytes 2506760 | tf_op jit(solution)/shard_map/ppermute | solution.py:108
  70.7 3.2 %collective-permute-start.21 = (bf16[4,272,384]{2,1,0:T(8,128)(2,1)}, bf16[4,272,384]{2,1,0:T(8,128)(2,1)}, u32[]{:S(2)}, u32[]{:S(2)}) collective-permute-start(bf16[4,272,384]{2,1,0:T(8,128)(2,1)} %collective-permute-done.10.rest_1_), channel_id=1, source_target_pairs={{0,1},{1,0},{2,3},{3,2},{4,5},{5,4},{6,7},{7,6},{8,9},{9,8},{10,11... | collective-permute-start | bytes 2506760 | tf_op jit(solution)/shard_map/ppermute | solution.py:108
  73.9 3.5 %collective-permute-done.18.after = bf16[64,1536]{1,0:T(8,128)(2,1)S(1)} collective-permute-done((bf16[64,1536]{1,0:T(8,128)(2,1)S(1)}, bf16[64,1536]{1,0:T(8,128)(2,1)S(1)}, u32[]{:S(2)}, u32[]{:S(2)}) %collective-permute-start.18) | collective-permute-done | bytes 196640 | tf_op jit(solution)/shard_map/ppermute | solution.py:108
  77.4 2.6 %shard_map.162.mixed = bf16[256,768]{1,0:T(8,128)(2,1)S(1)} custom-call(s32[66]{0:T(128)S(1)} %concatenate.67.place, bf16[256,768]{1,0:T(8,128)(2,1)S(1)} %get-tuple-element.55.query, bf16[256,1536]{1,0:T(8,128)(2,1)S(1)} %copy-done, bf16[64,1536]{1,0:T(8,128)(2,1)S(1)} %collective-permute-done.17.before, ...), custom_call_target="tpu_custom_call" | custom-call | bytes 11070000 | tf_op jit(solution)/shard_map/pallas_call | solution.py:331
  80.9 2.6 %collective-permute-done.23.rest_7_ = bf16[4,272,384]{2,1,0:T(8,128)(2,1)} collective-permute-done((bf16[4,272,384]{2,1,0:T(8,128)(2,1)}, bf16[4,272,384]{2,1,0:T(8,128)(2,1)}, u32[]{:S(2)}, u32[]{:S(2)}) %collective-permute-start.23) | collective-permute-done | bytes 835616 | tf_op jit(solution)/shard_map/ppermute | solution.py:108
  84.4 15.9 %shard_map.163 = (bf16[256,768]{1,0:T(8,128)(2,1)}, f32[256,768]{1,0:T(8,128)S(1)}, bf16[256,768]{1,0:T(8,128)(2,1)S(1)}, bf16[16,272,384]{2,1,0:T(8,128)(2,1)}, bf16[16,272,384]{2,1,0:T(8,128)(2,1)}) custom-call(s32[66]{0:T(128)S(1)} %concatenate.67.place, bf16[256,768]{1,0:T(8,128)(2,1)S(1)} %copy-done.1, bf16[256,768]{1,0:T(8,128)(2,1)S(1)} %shard_map.162.mixed, ...), custom_call_target="tpu_custom_call" | custom-call | bytes 51660000 | tf_op jit(solution)/shard_map/pallas_call | solution.py:331
  100.4 7.4 %shard_map.164 = (f32[256,768]{1,0:T(8,128)S(1)}, f32[256,1536]{1,0:T(8,128)S(1)}, bf16[64,1536]{1,0:T(8,128)(2,1)S(1)}, bf16[64,1536]{1,0:T(8,128)(2,1)S(1)}) custom-call(s32[66]{0:T(128)S(1)} %concatenate.67.place, bf16[256,768]{1,0:T(8,128)(2,1)S(1)} %get-tuple-element.55.query, bf16[256,1536]{1,0:T(8,128)(2,1)S(1)} %copy-done, ...), custom_call_target="tpu_custom_call" | custom-call | bytes 29520000 | tf_op jit(solution)/shard_map/pallas_call | solution.py:331
  107.8 2.3 %collective-permute-start.25 = (bf16[64,1536]{1,0:T(8,128)(2,1)S(1)}, bf16[64,1536]{1,0:T(8,128)(2,1)S(1)}, u32[]{:S(2)}, u32[]{:S(2)}) collective-permute-start(bf16[64,1536]{1,0:T(8,128)(2,1)S(1)} %get-tuple-element.67), channel_id=1, source_target_pairs={{1,0},{2,1},{3,2},{4,3},{5,4},{6,5},{7,6},{8,7},{9,8},{10,9},{11,1... | collective-permute-start | bytes 589832 | tf_op jit(solution)/shard_map/ppermute | solution.py:108
  110.2 3.2 %collective-permute-start.26 = (bf16[64,1536]{1,0:T(8,128)(2,1)S(1)}, bf16[64,1536]{1,0:T(8,128)(2,1)S(1)}, u32[]{:S(2)}, u32[]{:S(2)}) collective-permute-start(bf16[64,1536]{1,0:T(8,128)(2,1)S(1)} %get-tuple-element.68), channel_id=1, source_target_pairs={{0,1},{1,2},{2,3},{3,4},{4,5},{5,6},{6,7},{7,8},{8,9},{9,10},{10,1... | collective-permute-start | bytes 589832 | tf_op jit(solution)/shard_map/ppermute | solution.py:108
  113.4 2.9 %add.311 = bf16[16,272,384]{2,1,0:T(8,128)(2,1)S(1)} add(bf16[16,272,384]{2,1,0:T(8,128)(2,1)} %get-tuple-element.65, bf16[16,272,384]{2,1,0:T(8,128)(2,1)S(1)} %collective-permute-done.24) | non-fusion elementwise | flops 1671168 | bytes 10027008 | tf_op jit(solution)/shard_map/add | solution.py:619
  118.2 8.9 %shard_map.165 = (f32[256,768]{1,0:T(8,128)}, bf16[16,160,384]{2,1,0:T(8,128)(2,1)}, bf16[16,160,384]{2,1,0:T(8,128)(2,1)}) custom-call(s32[66]{0:T(128)S(1)} %concatenate.67.place, bf16[256,768]{1,0:T(8,128)(2,1)S(1)} %copy-done.1, bf16[256,768]{1,0:T(8,128)(2,1)S(1)} %copy-done.10, f32[1,768]{1,0:T(1,128)S(1)} %reshape.217.gain, ...), custom_call_target="tpu_custom_call" | custom-call | bytes 33210000 | tf_op jit(solution)/shard_map/pallas_call | solution.py:331
  127.1 10.6 %collective-permute-done.27 = bf16[8,272,384]{2,1,0:T(8,128)(2,1)S(1)} collective-permute-done((bf16[8,272,384]{2,1,0:T(8,128)(2,1)S(1)}, bf16[8,272,384]{2,1,0:T(8,128)(2,1)S(1)}, u32[]{:S(2)}, u32[]{:S(2)}) %collective-permute-start.27) | collective-permute-done | bytes 1671200 | tf_op jit(solution)/shard_map/ppermute | solution.py:108
  137.9 3.9 %collective-permute-start.28 = (bf16[16,160,384]{2,1,0:T(8,128)(2,1)S(1)}, bf16[16,160,384]{2,1,0:T(8,128)(2,1)S(1)}, u32[]{:S(2)}, u32[]{:S(2)}) collective-permute-start(bf16[16,160,384]{2,1,0:T(8,128)(2,1)S(1)} %copy-done.14), channel_id=1, source_target_pairs={{0,1},{1,0},{2,3},{3,2},{4,5},{5,4},{6,7},{7,6},{8,9},{9,8},{10,11... | collective-permute-start | bytes 5898248 | tf_op jit(solution)/shard_map/ppermute | solution.py:108
  142.2 3.3 %collective-permute-done.28 = bf16[16,160,384]{2,1,0:T(8,128)(2,1)S(1)} collective-permute-done((bf16[16,160,384]{2,1,0:T(8,128)(2,1)S(1)}, bf16[16,160,384]{2,1,0:T(8,128)(2,1)S(1)}, u32[]{:S(2)}, u32[]{:S(2)}) %collective-permute-start.28) | collective-permute-done | bytes 1966112 | tf_op jit(solution)/shard_map/ppermute | solution.py:108
  146.3 11.3 %collective-permute-done.29 = bf16[4,272,384]{2,1,0:T(8,128)(2,1)S(1)} collective-permute-done((bf16[4,272,384]{2,1,0:T(8,128)(2,1)S(1)}, bf16[4,272,384]{2,1,0:T(8,128)(2,1)S(1)}, u32[]{:S(2)}, u32[]{:S(2)}) %collective-permute-start.29) | collective-permute-done | bytes 835616 | tf_op jit(solution)/shard_map/ppermute | solution.py:108
  158.0 4.9 %collective-permute-done.30 = bf16[272,384]{1,0:T(8,128)(2,1)S(1)} collective-permute-done((bf16[272,384]{1,0:T(8,128)(2,1)S(1)}, bf16[272,384]{1,0:T(8,128)(2,1)S(1)}, u32[]{:S(2)}, u32[]{:S(2)}) %collective-permute-start.30) | collective-permute-done | bytes 208928 | tf_op jit(solution)/shard_map/ppermute | solution.py:108
  162.9 1.9 collective-permute-done.31
  165.3 1.9 collective-permute-start.33
  167.4 5.8 %collective-permute-done.32 = bf16[4,160,384]{2,1,0:T(8,128)(2,1)S(1)} collective-permute-done((bf16[4,160,384]{2,1,0:T(8,128)(2,1)S(1)}, bf16[4,160,384]{2,1,0:T(8,128)(2,1)S(1)}, u32[]{:S(2)}, u32[]{:S(2)}) %collective-permute-start.32) | collective-permute-done | bytes 491552 | tf_op jit(solution)/shard_map/ppermute | solution.py:108
  173.2 7.8 %collective-permute-done.33 = bf16[272,384]{1,0:T(8,128)(2,1)S(1)} collective-permute-done((bf16[272,384]{1,0:T(8,128)(2,1)S(1)}, bf16[272,384]{1,0:T(8,128)(2,1)S(1)}, u32[]{:S(2)}, u32[]{:S(2)}) %collective-permute-start.33) | collective-permute-done | bytes 208928 | tf_op jit(solution)/shard_map/ppermute | solution.py:108
  181.9 3.1 %collective-permute-start.37 = (bf16[160,384]{1,0:T(8,128)(2,1)S(1)}, bf16[160,384]{1,0:T(8,128)(2,1)S(1)}, u32[]{:S(2)}, u32[]{:S(2)}) collective-permute-start(bf16[160,384]{1,0:T(8,128)(2,1)S(1)} %get-tuple-element.104), channel_id=1, source_target_pairs={{0,16},{1,17},{2,18},{3,19},{4,20},{5,21},{6,22},{7,23},{8,24},{9,... | collective-permute-start | bytes 368648 | tf_op jit(solution)/shard_map/ppermute | solution.py:108
  189.1 4.0 %collective-permute-done.37 = bf16[160,384]{1,0:T(8,128)(2,1)S(1)} collective-permute-done((bf16[160,384]{1,0:T(8,128)(2,1)S(1)}, bf16[160,384]{1,0:T(8,128)(2,1)S(1)}, u32[]{:S(2)}, u32[]{:S(2)}) %collective-permute-start.37) | collective-permute-done | bytes 122912 | tf_op jit(solution)/shard_map/ppermute | solution.py:108
  193.0 3.7 %collective-permute-done.38 = bf16[160,384]{1,0:T(8,128)(2,1)S(1)} collective-permute-done((bf16[160,384]{1,0:T(8,128)(2,1)S(1)}, bf16[160,384]{1,0:T(8,128)(2,1)S(1)}, u32[]{:S(2)}, u32[]{:S(2)}) %collective-permute-start.38) | collective-permute-done | bytes 122912 | tf_op jit(solution)/shard_map/ppermute | solution.py:108
  (173 shorter events, 41.9 us)
Async XLA Ops:
  5.5 5.6 %collective-permute-start.4 = (bf16[128,384]{1,0:T(8,128)(2,1)S(1)}, bf16[128,384]{1,0:T(8,128)(2,1)S(1)}, u32[]{:S(2)}, u32[]{:S(2)}) collective-permute-start(bf16[128,384]{1,0:T(8,128)(2,1)S(1)} %pad_maximum_fusion.10), channel_id=1, source_target_pairs={{0,1},{1,0},{2,3},{3,2},{4,5},{5,4},{6,7},{7,6},{8,9},{9,8},{10,11... | collective-permute-start | bytes 294920 | tf_op jit(solution)/shard_map/ppermute | solution.py:108
  8.6 10.2 %collective-permute-start.2 = (bf16[160,384]{1,0:T(8,128)(2,1)S(1)}, bf16[160,384]{1,0:T(8,128)(2,1)S(1)}, u32[]{:S(2)}, u32[]{:S(2)}) collective-permute-start(bf16[160,384]{1,0:T(8,128)(2,1)S(1)} %get-tuple-element.124), channel_id=1, source_target_pairs={{0,16},{1,17},{2,18},{3,19},{4,20},{5,21},{6,22},{7,23},{8,24},{9,... | collective-permute-start | bytes 368648 | tf_op jit(solution)/shard_map/ppermute | solution.py:108
  9.7 11.6 %collective-permute-start.3 = (bf16[160,384]{1,0:T(8,128)(2,1)S(1)}, bf16[160,384]{1,0:T(8,128)(2,1)S(1)}, u32[]{:S(2)}, u32[]{:S(2)}) collective-permute-start(bf16[160,384]{1,0:T(8,128)(2,1)S(1)} %get-tuple-element.124), channel_id=1, source_target_pairs={{0,24},{1,25},{2,26},{3,27},{4,28},{5,29},{6,30},{7,31},{8,0},{9,1... | collective-permute-start | bytes 368648 | tf_op jit(solution)/shard_map/ppermute | solution.py:108
  21.4 11.9 %collective-permute-start.8 = (bf16[4,160,384]{2,1,0:T(8,128)(2,1)S(1)}, bf16[4,160,384]{2,1,0:T(8,128)(2,1)S(1)}, u32[]{:S(2)}, u32[]{:S(2)}) collective-permute-start(bf16[4,160,384]{2,1,0:T(8,128)(2,1)S(1)} %pad_maximum_fusion.1.rest_0_), channel_id=1, source_target_pairs={{0,4},{1,3},{2,6},{3,1},{4,0},{5,7},{6,2},{7,5},{8,12},{9,11},{10,... | collective-permute-start | bytes 1474568 | tf_op jit(solution)/shard_map/ppermute | solution.py:108
  22.6 25.2 %collective-permute-start.11 = (bf16[4,160,384]{2,1,0:T(8,128)(2,1)S(1)}, bf16[4,160,384]{2,1,0:T(8,128)(2,1)S(1)}, u32[]{:S(2)}, u32[]{:S(2)}) collective-permute-start(bf16[4,160,384]{2,1,0:T(8,128)(2,1)S(1)} %pad_maximum_fusion.1.rest_0_), channel_id=1, source_target_pairs={{0,2},{1,5},{2,0},{3,7},{4,6},{5,1},{6,4},{7,3},{8,10},{9,13},{10,... | collective-permute-start | bytes 1474568 | tf_op jit(solution)/shard_map/ppermute | solution.py:108
  22.9 12.9 %collective-permute-start.5 = (bf16[272,384]{1,0:T(8,128)(2,1)S(1)}, bf16[272,384]{1,0:T(8,128)(2,1)S(1)}, u32[]{:S(2)}, u32[]{:S(2)}) collective-permute-start(bf16[272,384]{1,0:T(8,128)(2,1)S(1)} %fusion.14), channel_id=1, source_target_pairs={{0,8},{1,9},{2,10},{3,11},{4,12},{5,13},{6,14},{7,15},{8,16},{9,17... | collective-permute-start | bytes 626696 | tf_op jit(solution)/shard_map/ppermute | solution.py:108
  22.9 17.1 %collective-permute-start.6 = (bf16[272,384]{1,0:T(8,128)(2,1)S(1)}, bf16[272,384]{1,0:T(8,128)(2,1)}, u32[]{:S(2)}, u32[]{:S(2)}) collective-permute-start(bf16[272,384]{1,0:T(8,128)(2,1)S(1)} %fusion.14), channel_id=1, source_target_pairs={{0,16},{1,17},{2,18},{3,19},{4,20},{5,21},{6,22},{7,23},{8,24},{9,... | collective-permute-start | bytes 626696 | tf_op jit(solution)/shard_map/ppermute | solution.py:108
  23.5 19.2 %collective-permute-start.7 = (bf16[272,384]{1,0:T(8,128)(2,1)S(1)}, bf16[272,384]{1,0:T(8,128)(2,1)}, u32[]{:S(2)}, u32[]{:S(2)}) collective-permute-start(bf16[272,384]{1,0:T(8,128)(2,1)S(1)} %fusion.14), channel_id=1, source_target_pairs={{0,24},{1,25},{2,26},{3,27},{4,28},{5,29},{6,30},{7,31},{8,0},{9,1... | collective-permute-start | bytes 626696 | tf_op jit(solution)/shard_map/ppermute | solution.py:108
  33.2 10.6 %collective-permute-start.9 = (bf16[4,160,384]{2,1,0:T(8,128)(2,1)S(1)}, bf16[4,160,384]{2,1,0:T(8,128)(2,1)}, u32[]{:S(2)}, u32[]{:S(2)}) collective-permute-start(bf16[4,160,384]{2,1,0:T(8,128)(2,1)S(1)} %collective-permute-done.8.rest_1_), channel_id=1, source_target_pairs={{0,2},{1,5},{2,0},{3,7},{4,6},{5,1},{6,4},{7,3},{8,10},{9,13},{10,... | collective-permute-start | bytes 1474568 | tf_op jit(solution)/shard_map/ppermute | solution.py:108
  35.8 14.4 %collective-permute-start.12 = (bf16[4,160,384]{2,1,0:T(8,128)(2,1)S(1)}, bf16[4,160,384]{2,1,0:T(8,128)(2,1)}, u32[]{:S(2)}, u32[]{:S(2)}) collective-permute-start(bf16[4,160,384]{2,1,0:T(8,128)(2,1)S(1)} %pad_maximum_fusion.1.rest_0_), channel_id=1, source_target_pairs={{0,1},{1,0},{2,3},{3,2},{4,5},{5,4},{6,7},{7,6},{8,9},{9,8},{10,11... | collective-permute-start | bytes 1474568 | tf_op jit(solution)/shard_map/ppermute | solution.py:108
  43.8 15.7 %collective-permute-start.10 = (bf16[4,272,384]{2,1,0:T(8,128)(2,1)S(1)}, bf16[4,272,384]{2,1,0:T(8,128)(2,1)}, u32[]{:S(2)}, u32[]{:S(2)}) collective-permute-start(bf16[4,272,384]{2,1,0:T(8,128)(2,1)S(1)} %pad_maximum_fusion.rest_0_), channel_id=1, source_target_pairs={{0,4},{1,3},{2,6},{3,1},{4,0},{5,7},{6,2},{7,5},{8,12},{9,11},{10,... | collective-permute-start | bytes 2506760 | tf_op jit(solution)/shard_map/ppermute | solution.py:108
  50.3 23.6 %collective-permute-start.19 = (bf16[4,272,384]{2,1,0:T(8,128)(2,1)S(1)}, bf16[4,272,384]{2,1,0:T(8,128)(2,1)}, u32[]{:S(2)}, u32[]{:S(2)}) collective-permute-start(bf16[4,272,384]{2,1,0:T(8,128)(2,1)S(1)} %pad_maximum_fusion.rest_0_), channel_id=1, source_target_pairs={{0,2},{1,5},{2,0},{3,7},{4,6},{5,1},{6,4},{7,3},{8,10},{9,13},{10,... | collective-permute-start | bytes 2506760 | tf_op jit(solution)/shard_map/ppermute | solution.py:108
  59.6 21.2 %collective-permute-start.16 = (bf16[4,272,384]{2,1,0:T(8,128)(2,1)}, bf16[4,272,384]{2,1,0:T(8,128)(2,1)}, u32[]{:S(2)}, u32[]{:S(2)}) collective-permute-start(bf16[4,272,384]{2,1,0:T(8,128)(2,1)} %collective-permute-done.10.rest_1_), channel_id=1, source_target_pairs={{0,2},{1,5},{2,0},{3,7},{4,6},{5,1},{6,4},{7,3},{8,10},{9,13},{10,... | collective-permute-start | bytes 2506760 | tf_op jit(solution)/shard_map/ppermute | solution.py:108
  61.4 9.3 %collective-permute-start.17 = (bf16[64,1536]{1,0:T(8,128)(2,1)S(1)}, bf16[64,1536]{1,0:T(8,128)(2,1)S(1)}, u32[]{:S(2)}, u32[]{:S(2)}) collective-permute-start(bf16[64,1536]{1,0:T(8,128)(2,1)S(1)} %get-tuple-element.101), channel_id=1, source_target_pairs={{0,1},{1,2},{2,3},{3,4},{4,5},{5,6},{6,7},{7,8},{8,9},{9,10},{10,1... | collective-permute-start | bytes 589832 | tf_op jit(solution)/shard_map/ppermute | solution.py:108
  65.8 11.6 %collective-permute-start.18 = (bf16[64,1536]{1,0:T(8,128)(2,1)S(1)}, bf16[64,1536]{1,0:T(8,128)(2,1)S(1)}, u32[]{:S(2)}, u32[]{:S(2)}) collective-permute-start(bf16[64,1536]{1,0:T(8,128)(2,1)S(1)} %get-tuple-element.100), channel_id=1, source_target_pairs={{1,0},{2,1},{3,2},{4,3},{5,4},{6,5},{7,6},{8,7},{9,8},{10,9},{11,1... | collective-permute-start | bytes 589832 | tf_op jit(solution)/shard_map/ppermute | solution.py:108
  68.0 12.8 %collective-permute-start.20 = (bf16[4,272,384]{2,1,0:T(8,128)(2,1)S(1)}, bf16[4,272,384]{2,1,0:T(8,128)(2,1)}, u32[]{:S(2)}, u32[]{:S(2)}) collective-permute-start(bf16[4,272,384]{2,1,0:T(8,128)(2,1)S(1)} %pad_maximum_fusion.rest_0_), channel_id=1, source_target_pairs={{0,1},{1,0},{2,3},{3,2},{4,5},{5,4},{6,7},{7,6},{8,9},{9,8},{10,11... | collective-permute-start | bytes 2506760 | tf_op jit(solution)/shard_map/ppermute | solution.py:108
  70.7 10.2 %collective-permute-start.21 = (bf16[4,272,384]{2,1,0:T(8,128)(2,1)}, bf16[4,272,384]{2,1,0:T(8,128)(2,1)}, u32[]{:S(2)}, u32[]{:S(2)}) collective-permute-start(bf16[4,272,384]{2,1,0:T(8,128)(2,1)} %collective-permute-done.10.rest_1_), channel_id=1, source_target_pairs={{0,1},{1,0},{2,3},{3,2},{4,5},{5,4},{6,7},{7,6},{8,9},{9,8},{10,11... | collective-permute-start | bytes 2506760 | tf_op jit(solution)/shard_map/ppermute | solution.py:108
  73.9 7.0 %collective-permute-start.22 = (bf16[4,272,384]{2,1,0:T(8,128)(2,1)}, bf16[4,272,384]{2,1,0:T(8,128)(2,1)}, u32[]{:S(2)}, u32[]{:S(2)}) collective-permute-start(bf16[4,272,384]{2,1,0:T(8,128)(2,1)} %collective-permute-done.19.rest_2_), channel_id=1, source_target_pairs={{0,1},{1,0},{2,3},{3,2},{4,5},{5,4},{6,7},{7,6},{8,9},{9,8},{10,11... | collective-permute-start | bytes 2506760 | tf_op jit(solution)/shard_map/ppermute | solution.py:108
  100.3 13.1 %collective-permute-start.24 = (bf16[16,272,384]{2,1,0:T(8,128)(2,1)}, bf16[16,272,384]{2,1,0:T(8,128)(2,1)S(1)}, u32[]{:S(2)}, u32[]{:S(2)}) collective-permute-start(bf16[16,272,384]{2,1,0:T(8,128)(2,1)} %get-tuple-element.66), channel_id=1, source_target_pairs={{0,1},{1,0},{2,3},{3,2},{4,5},{5,4},{6,7},{7,6},{8,9},{9,8},{10,11... | collective-permute-start | bytes 10027016 | tf_op jit(solution)/shard_map/ppermute | solution.py:108
  107.8 8.7 %collective-permute-start.25 = (bf16[64,1536]{1,0:T(8,128)(2,1)S(1)}, bf16[64,1536]{1,0:T(8,128)(2,1)S(1)}, u32[]{:S(2)}, u32[]{:S(2)}) collective-permute-start(bf16[64,1536]{1,0:T(8,128)(2,1)S(1)} %get-tuple-element.67), channel_id=1, source_target_pairs={{1,0},{2,1},{3,2},{4,3},{5,4},{6,5},{7,6},{8,7},{9,8},{10,9},{11,1... | collective-permute-start | bytes 589832 | tf_op jit(solution)/shard_map/ppermute | solution.py:108
  110.2 6.9 %collective-permute-start.26 = (bf16[64,1536]{1,0:T(8,128)(2,1)S(1)}, bf16[64,1536]{1,0:T(8,128)(2,1)S(1)}, u32[]{:S(2)}, u32[]{:S(2)}) collective-permute-start(bf16[64,1536]{1,0:T(8,128)(2,1)S(1)} %get-tuple-element.68), channel_id=1, source_target_pairs={{0,1},{1,2},{2,3},{3,4},{4,5},{5,6},{6,7},{7,8},{8,9},{9,10},{10,1... | collective-permute-start | bytes 589832 | tf_op jit(solution)/shard_map/ppermute | solution.py:108
  117.1 20.6 %collective-permute-start.27 = (bf16[8,272,384]{2,1,0:T(8,128)(2,1)S(1)}, bf16[8,272,384]{2,1,0:T(8,128)(2,1)S(1)}, u32[]{:S(2)}, u32[]{:S(2)}) collective-permute-start(bf16[8,272,384]{2,1,0:T(8,128)(2,1)S(1)} %slice.257), channel_id=1, source_target_pairs={{0,4},{1,3},{2,6},{3,1},{4,0},{5,7},{6,2},{7,5},{8,12},{9,11},{10,... | collective-permute-start | bytes 5013512 | tf_op jit(solution)/shard_map/ppermute | solution.py:108
  137.9 7.5 %collective-permute-start.28 = (bf16[16,160,384]{2,1,0:T(8,128)(2,1)S(1)}, bf16[16,160,384]{2,1,0:T(8,128)(2,1)S(1)}, u32[]{:S(2)}, u32[]{:S(2)}) collective-permute-start(bf16[16,160,384]{2,1,0:T(8,128)(2,1)S(1)} %copy-done.14), channel_id=1, source_target_pairs={{0,1},{1,0},{2,3},{3,2},{4,5},{5,4},{6,7},{7,6},{8,9},{9,8},{10,11... | collective-permute-start | bytes 5898248 | tf_op jit(solution)/shard_map/ppermute | solution.py:108
  142.0 15.6 %collective-permute-start.29 = (bf16[4,272,384]{2,1,0:T(8,128)(2,1)S(1)}, bf16[4,272,384]{2,1,0:T(8,128)(2,1)S(1)}, u32[]{:S(2)}, u32[]{:S(2)}) collective-permute-start(bf16[4,272,384]{2,1,0:T(8,128)(2,1)S(1)} %get-tuple-element.94), channel_id=1, source_target_pairs={{0,2},{1,5},{2,0},{3,7},{4,6},{5,1},{6,4},{7,3},{8,10},{9,13},{10,... | collective-permute-start | bytes 2506760 | tf_op jit(solution)/shard_map/ppermute | solution.py:108
  146.3 18.5 %collective-permute-start.31 = (bf16[8,160,384]{2,1,0:T(8,128)(2,1)S(1)}, bf16[8,160,384]{2,1,0:T(8,128)(2,1)S(1)}, u32[]{:S(2)}, u32[]{:S(2)}) collective-permute-start(bf16[8,160,384]{2,1,0:T(8,128)(2,1)S(1)} %get-tuple-element.92), channel_id=1, source_target_pairs={{0,4},{1,3},{2,6},{3,1},{4,0},{5,7},{6,2},{7,5},{8,12},{9,11},{10,... | collective-permute-start | bytes 2949128 | tf_op jit(solution)/shard_map/ppermute | solution.py:108
  165.1 8.0 %collective-permute-start.32 = (bf16[4,160,384]{2,1,0:T(8,128)(2,1)S(1)}, bf16[4,160,384]{2,1,0:T(8,128)(2,1)S(1)}, u32[]{:S(2)}, u32[]{:S(2)}) collective-permute-start(bf16[4,160,384]{2,1,0:T(8,128)(2,1)S(1)} %slice.264), channel_id=1, source_target_pairs={{0,2},{1,5},{2,0},{3,7},{4,6},{5,1},{6,4},{7,3},{8,10},{9,13},{10,... | collective-permute-start | bytes 1474568 | tf_op jit(solution)/shard_map/ppermute | solution.py:108
  165.3 15.7 %collective-permute-start.33 = (bf16[272,384]{1,0:T(8,128)(2,1)S(1)}, bf16[272,384]{1,0:T(8,128)(2,1)S(1)}, u32[]{:S(2)}, u32[]{:S(2)}) collective-permute-start(bf16[272,384]{1,0:T(8,128)(2,1)S(1)} %get-tuple-element.96), channel_id=1, source_target_pairs={{0,16},{1,17},{2,18},{3,19},{4,20},{5,21},{6,22},{7,23},{8,24},{9,... | collective-permute-start | bytes 626696 | tf_op jit(solution)/shard_map/ppermute | solution.py:108
  167.2 13.8 %collective-permute-start.34 = (bf16[272,384]{1,0:T(8,128)(2,1)S(1)}, bf16[272,384]{1,0:T(8,128)(2,1)S(1)}, u32[]{:S(2)}, u32[]{:S(2)}) collective-permute-start(bf16[272,384]{1,0:T(8,128)(2,1)S(1)} %get-tuple-element.97), channel_id=1, source_target_pairs={{0,24},{1,25},{2,26},{3,27},{4,28},{5,29},{6,30},{7,31},{8,0},{9,1... | collective-permute-start | bytes 626696 | tf_op jit(solution)/shard_map/ppermute | solution.py:108
  181.3 5.2 %collective-permute-start.35 = (f32[128,384]{1,0:T(8,128)S(1)}, f32[128,384]{1,0:T(8,128)S(1)}, u32[]{:S(2)}, u32[]{:S(2)}) collective-permute-start(f32[128,384]{1,0:T(8,128)S(1)} %pad_maximum_fusion.2), channel_id=1, source_target_pairs={{0,1},{1,0},{2,3},{3,2},{4,5},{5,4},{6,7},{7,6},{8,9},{9,8},{10,11... | collective-permute-start | bytes 589832 | tf_op jit(solution)/shard_map/ppermute | solution.py:108
  181.9 7.2 %collective-permute-start.36 = (bf16[160,384]{1,0:T(8,128)(2,1)S(1)}, bf16[160,384]{1,0:T(8,128)(2,1)S(1)}, u32[]{:S(2)}, u32[]{:S(2)}) collective-permute-start(bf16[160,384]{1,0:T(8,128)(2,1)S(1)} %get-tuple-element.105), channel_id=1, source_target_pairs={{0,8},{1,9},{2,10},{3,11},{4,12},{5,13},{6,14},{7,15},{8,16},{9,17... | collective-permute-start | bytes 368648 | tf_op jit(solution)/shard_map/ppermute | solution.py:108
  181.9 11.1 %collective-permute-start.37 = (bf16[160,384]{1,0:T(8,128)(2,1)S(1)}, bf16[160,384]{1,0:T(8,128)(2,1)S(1)}, u32[]{:S(2)}, u32[]{:S(2)}) collective-permute-start(bf16[160,384]{1,0:T(8,128)(2,1)S(1)} %get-tuple-element.104), channel_id=1, source_target_pairs={{0,16},{1,17},{2,18},{3,19},{4,20},{5,21},{6,22},{7,23},{8,24},{9,... | collective-permute-start | bytes 368648 | tf_op jit(solution)/shard_map/ppermute | solution.py:108
  185.1 11.7 %collective-permute-start.38 = (bf16[160,384]{1,0:T(8,128)(2,1)S(1)}, bf16[160,384]{1,0:T(8,128)(2,1)S(1)}, u32[]{:S(2)}, u32[]{:S(2)}) collective-permute-start(bf16[160,384]{1,0:T(8,128)(2,1)S(1)} %get-tuple-element.103), channel_id=1, source_target_pairs={{0,24},{1,25},{2,26},{3,27},{4,28},{5,29},{6,30},{7,31},{8,0},{9,1... | collective-permute-start | bytes 368648 | tf_op jit(solution)/shard_map/ppermute | solution.py:108
  (24 other events, 199.5 us)
